TPU v7x, 256 devices: a whole 4x4x8 slice. The times are simulated.
256 devices in a mesh: blk: 8 (over z), col: 32 (over y, x, core).
Axes of the slice: x: 4, y: 4, z: 8, core: 2. Of those that a mesh axis runs over, the one named last changes fastest.
Arguments:
- loads: bfloat16 [65536, 256], P('col'), may hold values from -6 to 6
- dense_blocks: bfloat16 [8, 32, 60, 256, 256], P('blk', 'col'), may hold values from -0.046875 to 0.046875
- dense_source: int32 [8, 32, 60], P('blk', 'col'), may hold values from 0 to 7
- dense_target: int32 [8, 32, 60], P('blk', 'col'), may hold values from 0 to 31
- left_factors: bfloat16 [8, 32, 64, 32, 256], P('blk', 'col'), may hold values from -0.375 to 0.375
- right_factors: bfloat16 [8, 32, 64, 32, 256], P('blk', 'col'), may hold values from -0.125 to 0.125
- block_owner: int32 [8, 32, 64, 1], P(None, 'col'), may hold values from 0 to 7; in each aligned block of 64 rows (0 to 63, 64 to 127, ..., all dimensions but the last counted through in order) at most 16 rows name the same one
- block_source: int32 [8, 32, 64], P(None, 'col'), may hold values from 0 to 7
- block_target: int32 [8, 32, 64], P(None, 'col'), may hold values from 0 to 31
Outputs:
- adjoint: bfloat16 [65536, 256], P(('blk', 'col'))
Inputs may be any that keep to these rules, and one draw needn't show every extreme that they name: `block_owner`: among the 64 blocks stored on one device no owner is named more than 16 times.
All inputs are finite; a program needn't handle non-finite values.
Results may differ from a plain program's by a relative error of at most 0.0039.
Values may be sent and summed in bfloat16 or wider, within the bound.
A program may use at most 128 MiB of HBM per device.

v0:
```python
from functools import partial

import jax
import jax.numpy as jnp
from jax import lax
from jax.sharding import PartitionSpec as P

LEAF = 256
CASES = 256
SC_DEV = 8
TC_PER = 1
LR_DEV = 64


def slot_tables(owners, destinations, capacity):
    targets_all = jnp.arange(destinations, dtype=jnp.int32)
    matched = (owners[:, None] == targets_all[None, :]).astype(jnp.int32)
    ranking = jnp.sum((jnp.cumsum(matched, axis=0) - 1) * matched, axis=1)
    places = jnp.arange(capacity, dtype=jnp.int32)
    chosen = (owners[None, None, :] == targets_all[:, None, None]) & (
        ranking[None, None, :] == places[None, :, None]
    )
    blocks = jnp.arange(owners.shape[0], dtype=jnp.int32)
    position = jnp.sum(jnp.where(chosen, blocks[None, None, :], 0), axis=2)
    filled = jnp.any(chosen, axis=2)
    return (position, filled)


def cluster_total(target_ids, number, terms):
    wanted = jnp.arange(number, dtype=jnp.int32)
    selector = (target_ids[None, :] == wanted[:, None]).astype(jnp.float32)
    return jnp.einsum("tn,njr->tjr", selector, terms, precision=lax.Precision.HIGHEST)


def shards(
    loads,
    dense_blocks,
    dense_source,
    dense_target,
    left_factors,
    right_factors,
    block_owner,
    block_source,
    block_target,
):
    senders = lax.axis_size("blk")
    own_index = lax.axis_index("blk")
    clusters = TC_PER * lax.axis_size("col")
    capacity = LR_DEV // 4
    source_group = loads.reshape(SC_DEV, LEAF, CASES)
    owners = block_owner[:, 0, :, 0]
    sources = block_source[:, 0]
    targets = block_target[:, 0]
    tables, filled = jax.vmap(partial(slot_tables, destinations=senders, capacity=capacity))(owners)
    send_position = lax.dynamic_index_in_dim(tables, own_index, 0, keepdims=False)
    send_filled = lax.dynamic_index_in_dim(filled, own_index, 0, keepdims=False)
    recv_position = lax.dynamic_index_in_dim(tables, own_index, 1, keepdims=False)
    recv_filled = lax.dynamic_index_in_dim(filled, own_index, 1, keepdims=False)
    recv_sources = jnp.take_along_axis(sources, recv_position, axis=1)
    recv_targets = jnp.where(
        recv_filled, jnp.take_along_axis(targets, recv_position, axis=1), clusters
    )
    accumulated = jnp.zeros((clusters, LEAF, CASES), jnp.float32)
    slot_mask = send_filled[:, :, None, None]
    zero_value = jnp.zeros((), jnp.bfloat16)
    right_sent = jnp.where(slot_mask, right_factors[0, 0][send_position], zero_value)
    left_sent = jnp.where(slot_mask, left_factors[0, 0][send_position], zero_value)
    received = (
        lax.all_to_all(left_sent, "blk", split_axis=0, concat_axis=0, tiled=True),
        lax.all_to_all(right_sent, "blk", split_axis=0, concat_axis=0, tiled=True),
    )

    def add_sender(accumulated, current):
        left_panels, right_panels, source_ids, target_ids = current
        picked_rows = source_group[source_ids]
        coefficients = jnp.einsum(
            "nki,nir->nkr", left_panels, picked_rows, preferred_element_type=jnp.float32
        ).astype(jnp.bfloat16)
        contributions = jnp.einsum(
            "nki,nkr->nir", right_panels, coefficients, preferred_element_type=jnp.float32
        )
        return (accumulated + cluster_total(target_ids, clusters, contributions), None)

    accumulated, unused = lax.scan(
        add_sender, accumulated, (received[0], received[1], recv_sources, recv_targets)
    )
    dense_targets = dense_target[0, 0]
    dense_panels = dense_blocks[0, 0]
    dense_picked = source_group[dense_source[0, 0]]
    dense_terms = jnp.einsum(
        "nij,nir->njr", dense_panels, dense_picked, preferred_element_type=jnp.float32
    )
    accumulated = accumulated + cluster_total(dense_targets, clusters, dense_terms)
    summed = lax.psum_scatter(
        accumulated.reshape(clusters * LEAF, CASES), "col", scatter_dimension=0, tiled=True
    )
    return summed.astype(jnp.bfloat16)


def solution(mesh):
    placed = (
        P("col", None),
        P("blk", "col", None, None, None),
        P("blk", "col", None),
        P("blk", "col", None),
        P("blk", "col", None, None, None),
        P("blk", "col", None, None, None),
        P(None, "col", None, None),
        P(None, "col", None),
        P(None, "col", None),
    )
    return jax.shard_map(
        shards, mesh=mesh, in_specs=placed, out_specs=P(("blk", "col"), None), check_vma=False
    )
```

profile of v0, /device:TPU:1, one launch (start us, length us, event | category | flops | bytes accessed | tf_op | source)
XLA Modules:
  0.0 395.9 jit_solution(2357892887458830169)
XLA Ops:
  6.5 0.9 copy.26
  7.4 0.7 iota_compare_fusion.4
  8.1 1.3 fusion.28
  9.4 0.1 copy.27
  9.5 1.2 fusion.21
  10.7 1.2 and_reduce_fusion
  11.9 0.1 reshape.143
  12.0 0.7 gather_fusion.1
  12.6 3.2 gather_fusion.2
  15.9 3.3 broadcast_select_fusion
  19.2 58.7 %all_to_all.10 = bf16[8,16,32,256]{3,2,1,0:T(8,128)(2,1)} all-to-all(bf16[8,16,32,256]{3,2,1,0:T(8,128)(2,1)S(1)} %get-tuple-element.85), channel_id=1, replica_groups=mesh['blk'=8,'col'=32] {'blk'}, dimensions={0} | all-to-all | bytes 4194304 | tf_op jit(solution)/shard_map/all_to_all | solution.py:70
  77.9 3.7 all-to-all-start.1
  81.6 0.2 reduce-scatter.2.cloned.1.call-start
  81.9 0.1 reshape.181
  82.0 0.0 copy-start.4
  82.0 1.0 gather_fusion.5
  83.0 0.1 reshape.189
  83.1 1.0 gather_fusion.4
  84.1 0.1 reshape.184
  84.2 5.4 %gather_fusion.3 = bf16[60,256,256]{2,1,0:T(8,128)(2,1)} fusion(bf16[8,256,256]{2,1,0:T(8,128)(2,1)S(1)} %bitcast.76, s32[1024]{0:T(1024)S(1)} %pad_clamp_fusion.1), kind=kCustom, calls=%fused_computation.5 | custom fusion | bytes 15728880 | tf_op jit(solution)/shard_map/gather | solution.py:89
  89.6 13.2 %convolution_bitcast_fusion = f32[60,256,256]{1,2,0:T(8,128)} fusion(bf16[60,256,256]{2,1,0:T(8,128)(2,1)} %gather_fusion.3, bf16[1,1,60,256,256]{4,3,2,1,0:T(8,128)(2,1)} %param.14), kind=kOutput, calls=%fused_computation.26 | convolution fusion | flops 2013265920 | bytes 31457280 | tf_op jit(solution)/shard_map/nij,nir->njr/dot_general | solution.py:90
  102.9 17.1 %copy.29 = f32[60,256,256]{2,0,1:T(8,128)} copy(f32[60,256,256]{1,2,0:T(8,128)} %convolution_bitcast_fusion) | data formatting | bytes 31457280 | tf_op jit(solution)/shard_map/nij,nir->njr/dot_general | solution.py:90
  120.0 13.3 %all-to-all-done.1 = bf16[8,16,32,256]{3,2,1,0:T(8,128)(2,1)S(1)} async-done(((bf16[8,16,32,256]{3,2,1,0:T(8,128)(2,1)}), bf16[8,16,32,256]{3,2,1,0:T(8,128)(2,1)S(1)}, u32[]{:S(2)}, u32[]{:S(2)}) %all-to-all-start.1) | async-done | bytes 2097184 | tf_op jit(solution)/shard_map/all_to_all | solution.py:69
  133.2 139.0 %while.11 = (s32[]{:T(128)}, f32[32,256,256]{2,0,1:T(8,128)}, s32[8,16]{1,0:T(8,128)S(1)}, bf16[8,16,32,256]{3,2,1,0:T(8,128)(2,1)}, bf16[8,16,32,256]{3,2,1,0:T...) while((s32[]{:T(128)}, f32[32,256,256]{2,0,1:T(8,128)}, ...), condition=%wide.region_5.7_spmd.clone, body=%wide.region_4.6_spmd.clone.sunk | while | flops 541197888 | bytes 48764516 | solution.py:84
  133.3 1.3 copy-done.5
  134.5 0.7 gather_fusion
  135.2 4.0 %fusion.46 = f32[16,256,256]{2,1,0:T(8,128)} fusion(bf16[16,256,256]{2,1,0:T(8,128)(2,1)S(1)} %gather_fusion, bf16[8,16,32,256]{3,2,1,0:T(8,128)(2,1)} %copy-done.5, s32[]{:T(128)} %get-tuple-element.138, bf16[8,16,32,256]{3,2,1,0:T(8,128)(2,1)} %get-tuple-element.150), kind=kOutput, calls=%fused_computation.10.clone.1 | convolution fusion | flops 134348800 | bytes 6816768 | tf_op jit(solution)/shard_map/while/body/eval_jaxpr/nki,nkr->nir/dot_general | solution.py:79
  139.2 10.3 %select_add_fusion.2 = f32[32,256,256]{2,0,1:T(8,128)} fusion(f32[32,256,256]{2,0,1:T(8,128)} %get-tuple-element.139, pred[]{:T(512)S(6)} %compare.3, f32[16,256,256]{2,1,0:T(8,128)} %fusion.46, s32[16]{0:T(128)S(1)} %fusion.47), kind=kOutput, calls=%fused_computation.6.clone.1 | convolution fusion | flops 406848000 | bytes 20971584 | tf_op jit(solution)/shard_map/while/body/eval_jaxpr/tn,njr->tjr/dot_general | solution.py:32
  149.6 1.3 copy-done.5
  150.8 0.7 gather_fusion
  151.5 4.0 %fusion.46 = f32[16,256,256]{2,1,0:T(8,128)} fusion(bf16[16,256,256]{2,1,0:T(8,128)(2,1)S(1)} %gather_fusion, bf16[8,16,32,256]{3,2,1,0:T(8,128)(2,1)} %copy-done.5, s32[]{:T(128)} %get-tuple-element.138, bf16[8,16,32,256]{3,2,1,0:T(8,128)(2,1)} %get-tuple-element.150), kind=kOutput, calls=%fused_computation.10.clone.1 | convolution fusion | flops 134348800 | bytes 6816768 | tf_op jit(solution)/shard_map/while/body/eval_jaxpr/nki,nkr->nir/dot_general | solution.py:79
  155.5 11.6 %select_add_fusion.2 = f32[32,256,256]{2,0,1:T(8,128)} fusion(f32[32,256,256]{2,0,1:T(8,128)} %get-tuple-element.139, pred[]{:T(512)S(6)} %compare.3, f32[16,256,256]{2,1,0:T(8,128)} %fusion.46, s32[16]{0:T(128)S(1)} %fusion.47), kind=kOutput, calls=%fused_computation.6.clone.1 | convolution fusion | flops 406848000 | bytes 20971584 | tf_op jit(solution)/shard_map/while/body/eval_jaxpr/tn,njr->tjr/dot_general | solution.py:32
  167.1 0.0 copy-done.6
  167.1 1.3 copy-done.5
  168.4 0.7 gather_fusion
  169.1 4.0 %fusion.46 = f32[16,256,256]{2,1,0:T(8,128)} fusion(bf16[16,256,256]{2,1,0:T(8,128)(2,1)S(1)} %gather_fusion, bf16[8,16,32,256]{3,2,1,0:T(8,128)(2,1)} %copy-done.5, s32[]{:T(128)} %get-tuple-element.138, bf16[8,16,32,256]{3,2,1,0:T(8,128)(2,1)} %get-tuple-element.150), kind=kOutput, calls=%fused_computation.10.clone.1 | convolution fusion | flops 134348800 | bytes 6816768 | tf_op jit(solution)/shard_map/while/body/eval_jaxpr/nki,nkr->nir/dot_general | solution.py:79
  173.0 11.5 %select_add_fusion.2 = f32[32,256,256]{2,0,1:T(8,128)} fusion(f32[32,256,256]{2,0,1:T(8,128)} %get-tuple-element.139, pred[]{:T(512)S(6)} %compare.3, f32[16,256,256]{2,1,0:T(8,128)} %fusion.46, s32[16]{0:T(128)S(1)} %fusion.47), kind=kOutput, calls=%fused_computation.6.clone.1 | convolution fusion | flops 406848000 | bytes 20971584 | tf_op jit(solution)/shard_map/while/body/eval_jaxpr/tn,njr->tjr/dot_general | solution.py:32
  184.6 1.3 copy-done.5
  185.9 0.7 gather_fusion
  186.6 4.0 %fusion.46 = f32[16,256,256]{2,1,0:T(8,128)} fusion(bf16[16,256,256]{2,1,0:T(8,128)(2,1)S(1)} %gather_fusion, bf16[8,16,32,256]{3,2,1,0:T(8,128)(2,1)} %copy-done.5, s32[]{:T(128)} %get-tuple-element.138, bf16[8,16,32,256]{3,2,1,0:T(8,128)(2,1)} %get-tuple-element.150), kind=kOutput, calls=%fused_computation.10.clone.1 | convolution fusion | flops 134348800 | bytes 6816768 | tf_op jit(solution)/shard_map/while/body/eval_jaxpr/nki,nkr->nir/dot_general | solution.py:79
  190.6 11.6 %select_add_fusion.2 = f32[32,256,256]{2,0,1:T(8,128)} fusion(f32[32,256,256]{2,0,1:T(8,128)} %get-tuple-element.139, pred[]{:T(512)S(6)} %compare.3, f32[16,256,256]{2,1,0:T(8,128)} %fusion.46, s32[16]{0:T(128)S(1)} %fusion.47), kind=kOutput, calls=%fused_computation.6.clone.1 | convolution fusion | flops 406848000 | bytes 20971584 | tf_op jit(solution)/shard_map/while/body/eval_jaxpr/tn,njr->tjr/dot_general | solution.py:32
  202.2 1.3 copy-done.5
  203.4 0.7 gather_fusion
  204.1 4.0 %fusion.46 = f32[16,256,256]{2,1,0:T(8,128)} fusion(bf16[16,256,256]{2,1,0:T(8,128)(2,1)S(1)} %gather_fusion, bf16[8,16,32,256]{3,2,1,0:T(8,128)(2,1)} %copy-done.5, s32[]{:T(128)} %get-tuple-element.138, bf16[8,16,32,256]{3,2,1,0:T(8,128)(2,1)} %get-tuple-element.150), kind=kOutput, calls=%fused_computation.10.clone.1 | convolution fusion | flops 134348800 | bytes 6816768 | tf_op jit(solution)/shard_map/while/body/eval_jaxpr/nki,nkr->nir/dot_general | solution.py:79
  208.1 11.5 %select_add_fusion.2 = f32[32,256,256]{2,0,1:T(8,128)} fusion(f32[32,256,256]{2,0,1:T(8,128)} %get-tuple-element.139, pred[]{:T(512)S(6)} %compare.3, f32[16,256,256]{2,1,0:T(8,128)} %fusion.46, s32[16]{0:T(128)S(1)} %fusion.47), kind=kOutput, calls=%fused_computation.6.clone.1 | convolution fusion | flops 406848000 | bytes 20971584 | tf_op jit(solution)/shard_map/while/body/eval_jaxpr/tn,njr->tjr/dot_general | solution.py:32
  219.7 1.3 copy-done.5
  221.0 0.7 gather_fusion
  221.7 4.0 %fusion.46 = f32[16,256,256]{2,1,0:T(8,128)} fusion(bf16[16,256,256]{2,1,0:T(8,128)(2,1)S(1)} %gather_fusion, bf16[8,16,32,256]{3,2,1,0:T(8,128)(2,1)} %copy-done.5, s32[]{:T(128)} %get-tuple-element.138, bf16[8,16,32,256]{3,2,1,0:T(8,128)(2,1)} %get-tuple-element.150), kind=kOutput, calls=%fused_computation.10.clone.1 | convolution fusion | flops 134348800 | bytes 6816768 | tf_op jit(solution)/shard_map/while/body/eval_jaxpr/nki,nkr->nir/dot_general | solution.py:79
  225.6 11.5 %select_add_fusion.2 = f32[32,256,256]{2,0,1:T(8,128)} fusion(f32[32,256,256]{2,0,1:T(8,128)} %get-tuple-element.139, pred[]{:T(512)S(6)} %compare.3, f32[16,256,256]{2,1,0:T(8,128)} %fusion.46, s32[16]{0:T(128)S(1)} %fusion.47), kind=kOutput, calls=%fused_computation.6.clone.1 | convolution fusion | flops 406848000 | bytes 20971584 | tf_op jit(solution)/shard_map/while/body/eval_jaxpr/tn,njr->tjr/dot_general | solution.py:32
  237.2 1.3 copy-done.5
  238.5 0.7 gather_fusion
  239.2 4.0 %fusion.46 = f32[16,256,256]{2,1,0:T(8,128)} fusion(bf16[16,256,256]{2,1,0:T(8,128)(2,1)S(1)} %gather_fusion, bf16[8,16,32,256]{3,2,1,0:T(8,128)(2,1)} %copy-done.5, s32[]{:T(128)} %get-tuple-element.138, bf16[8,16,32,256]{3,2,1,0:T(8,128)(2,1)} %get-tuple-element.150), kind=kOutput, calls=%fused_computation.10.clone.1 | convolution fusion | flops 134348800 | bytes 6816768 | tf_op jit(solution)/shard_map/while/body/eval_jaxpr/nki,nkr->nir/dot_general | solution.py:79
  243.2 11.6 %select_add_fusion.2 = f32[32,256,256]{2,0,1:T(8,128)} fusion(f32[32,256,256]{2,0,1:T(8,128)} %get-tuple-element.139, pred[]{:T(512)S(6)} %compare.3, f32[16,256,256]{2,1,0:T(8,128)} %fusion.46, s32[16]{0:T(128)S(1)} %fusion.47), kind=kOutput, calls=%fused_computation.6.clone.1 | convolution fusion | flops 406848000 | bytes 20971584 | tf_op jit(solution)/shard_map/while/body/eval_jaxpr/tn,njr->tjr/dot_general | solution.py:32
  254.7 0.0 copy-done.6
  254.8 1.3 copy-done.5
  256.0 0.7 gather_fusion
  256.7 4.0 %fusion.46 = f32[16,256,256]{2,1,0:T(8,128)} fusion(bf16[16,256,256]{2,1,0:T(8,128)(2,1)S(1)} %gather_fusion, bf16[8,16,32,256]{3,2,1,0:T(8,128)(2,1)} %copy-done.5, s32[]{:T(128)} %get-tuple-element.138, bf16[8,16,32,256]{3,2,1,0:T(8,128)(2,1)} %get-tuple-element.150), kind=kOutput, calls=%fused_computation.10.clone.1 | convolution fusion | flops 134348800 | bytes 6816768 | tf_op jit(solution)/shard_map/while/body/eval_jaxpr/nki,nkr->nir/dot_general | solution.py:79
  260.7 11.5 %select_add_fusion.2 = f32[32,256,256]{2,0,1:T(8,128)} fusion(f32[32,256,256]{2,0,1:T(8,128)} %get-tuple-element.139, pred[]{:T(512)S(6)} %compare.3, f32[16,256,256]{2,1,0:T(8,128)} %fusion.46, s32[16]{0:T(128)S(1)} %fusion.47), kind=kOutput, calls=%fused_computation.6.clone.1 | convolution fusion | flops 406848000 | bytes 20971584 | tf_op jit(solution)/shard_map/while/body/eval_jaxpr/tn,njr->tjr/dot_general | solution.py:32
  272.3 12.1 %convolution_add_fusion = f32[32,256,256]{2,0,1:T(8,128)S(1)} fusion(f32[32,256,256]{2,0,1:T(8,128)} %get-tuple-element.43, f32[60,256,256]{2,0,1:T(8,128)} %copy.29, s32[60]{0:T(128)S(1)} %bitcast.86), kind=kOutput, calls=%fused_computation.28 | convolution fusion | flops 1512048512 | bytes 32506096 | tf_op jit(solution)/shard_map/tn,njr->tjr/dot_general | solution.py:32
  284.4 8.1 %copy.30 = f32[32,256,256]{2,1,0:T(8,128)} copy(f32[32,256,256]{2,0,1:T(8,128)S(1)} %convolution_add_fusion) | data formatting | bytes 16777216 | tf_op jit(solution)/shard_map/add | solution.py:93
  292.4 0.0 reduce-scatter.2.cloned.1.call-update
  292.5 95.0 %reduce-scatter.2.cloned.1.call-done = f32[256,256]{1,0:T(8,128)} async-done(((f32[8192,256]{1,0:T(8,128)}), f32[256,256]{1,0:T(8,128)}) %reduce-scatter.2.cloned.1.call-update) | async-done | bytes 262160 | tf_op jit(solution)/shard_map/reduce_scatter | solution.py:94
  387.4 1.6 convert_element_type.12
  389.1 0.0 copy-done.1
  (70 shorter events, 0.3 us)
Async XLA Ops:
  6.5 5.4 %copy-start = (bf16[1,1,64,32,256]{4,3,2,1,0:T(8,128)(2,1)S(1)}, bf16[1,1,64,32,256]{4,3,2,1,0:T(8,128)(2,1)}, u32[]{:S(2)}) copy-start(bf16[1,1,64,32,256]{4,3,2,1,0:T(8,128)(2,1)} %param.18) | copy-start | bytes 3145732
  19.2 62.8 %copy-start.2 = (s32[8,1,64]{2,1,0:T(1,128)S(1)}, s32[8,1,64]{2,1,0:T(1,128)}, u32[]{:S(2)}) copy-start(s32[8,1,64]{2,1,0:T(1,128)} %param.20) | copy-start | bytes 6148
  77.9 5.2 %copy-start.3 = (s32[8,1,64]{2,1,0:T(1,128)S(1)}, s32[8,1,64]{2,1,0:T(1,128)}, u32[]{:S(2)}) copy-start(s32[8,1,64]{2,1,0:T(1,128)} %param.21) | copy-start | bytes 6148
  77.9 55.3 %all-to-all-start.1 = ((bf16[8,16,32,256]{3,2,1,0:T(8,128)(2,1)}), bf16[8,16,32,256]{3,2,1,0:T(8,128)(2,1)S(1)}, u32[]{:S(2)}, u32[]{:S(2)}) async-start(bf16[8,16,32,256]{3,2,1,0:T(8,128)(2,1)} %get-tuple-element.84), calls=%async_computation.1 | async-start | bytes 4194304 | tf_op jit(solution)/shard_map/all_to_all | solution.py:69
  81.6 305.8 %reduce-scatter.2.cloned.1.call-start = ((), (), s32[]{:S(2)}) async-start(), calls=%async_computation.3 | async-start | bytes 8650752 | tf_op jit(solution)/shard_map/reduce_scatter | solution.py:94
  82.0 2.2 copy-start.8
  82.0 2.2 copy-start.4
  133.2 139.0 %copy-start.7 = (s32[1,1,60]{2,1,0:T(1,128)S(1)}, s32[1,1,60]{2,1,0:T(1,128)}, u32[]{:S(2)}) copy-start(s32[1,1,60]{2,1,0:T(1,128)} %param.16) | copy-start | bytes 724
  133.2 1.3 copy-start.5
  139.2 10.3 %copy-start.6 = (bf16[8,16,32,256]{3,2,1,0:T(8,128)(2,1)S(1)}, bf16[8,16,32,256]{3,2,1,0:T(8,128)(2,1)}, u32[]{:S(2)}) copy-start(bf16[8,16,32,256]{3,2,1,0:T(8,128)(2,1)} %copy-done.5) | copy-start | bytes 6291460 | tf_op jit(solution)/shard_map/while
  149.5 1.3 copy-start.5
  155.5 11.6 %copy-start.6 = (bf16[8,16,32,256]{3,2,1,0:T(8,128)(2,1)S(1)}, bf16[8,16,32,256]{3,2,1,0:T(8,128)(2,1)}, u32[]{:S(2)}) copy-start(bf16[8,16,32,256]{3,2,1,0:T(8,128)(2,1)} %copy-done.5) | copy-start | bytes 6291460 | tf_op jit(solution)/shard_map/while
  167.1 1.3 copy-start.5
  173.0 11.6 %copy-start.6 = (bf16[8,16,32,256]{3,2,1,0:T(8,128)(2,1)S(1)}, bf16[8,16,32,256]{3,2,1,0:T(8,128)(2,1)}, u32[]{:S(2)}) copy-start(bf16[8,16,32,256]{3,2,1,0:T(8,128)(2,1)} %copy-done.5) | copy-start | bytes 6291460 | tf_op jit(solution)/shard_map/while
  184.6 1.3 copy-start.5
  190.6 11.6 %copy-start.6 = (bf16[8,16,32,256]{3,2,1,0:T(8,128)(2,1)S(1)}, bf16[8,16,32,256]{3,2,1,0:T(8,128)(2,1)}, u32[]{:S(2)}) copy-start(bf16[8,16,32,256]{3,2,1,0:T(8,128)(2,1)} %copy-done.5) | copy-start | bytes 6291460 | tf_op jit(solution)/shard_map/while
  202.1 1.3 copy-start.5
  208.1 11.6 %copy-start.6 = (bf16[8,16,32,256]{3,2,1,0:T(8,128)(2,1)S(1)}, bf16[8,16,32,256]{3,2,1,0:T(8,128)(2,1)}, u32[]{:S(2)}) copy-start(bf16[8,16,32,256]{3,2,1,0:T(8,128)(2,1)} %copy-done.5) | copy-start | bytes 6291460 | tf_op jit(solution)/shard_map/while
  219.7 1.3 copy-start.5
  225.6 11.6 %copy-start.6 = (bf16[8,16,32,256]{3,2,1,0:T(8,128)(2,1)S(1)}, bf16[8,16,32,256]{3,2,1,0:T(8,128)(2,1)}, u32[]{:S(2)}) copy-start(bf16[8,16,32,256]{3,2,1,0:T(8,128)(2,1)} %copy-done.5) | copy-start | bytes 6291460 | tf_op jit(solution)/shard_map/while
  237.2 1.3 copy-start.5
  243.2 11.6 %copy-start.6 = (bf16[8,16,32,256]{3,2,1,0:T(8,128)(2,1)S(1)}, bf16[8,16,32,256]{3,2,1,0:T(8,128)(2,1)}, u32[]{:S(2)}) copy-start(bf16[8,16,32,256]{3,2,1,0:T(8,128)(2,1)} %copy-done.5) | copy-start | bytes 6291460 | tf_op jit(solution)/shard_map/while
  254.7 1.3 copy-start.5
  260.7 11.6 %copy-start.6 = (bf16[8,16,32,256]{3,2,1,0:T(8,128)(2,1)S(1)}, bf16[8,16,32,256]{3,2,1,0:T(8,128)(2,1)}, u32[]{:S(2)}) copy-start(bf16[8,16,32,256]{3,2,1,0:T(8,128)(2,1)} %copy-done.5) | copy-start | bytes 6291460 | tf_op jit(solution)/shard_map/while
  292.4 96.6 %copy-start.1 = (bf16[1,1,64,32,256]{4,3,2,1,0:T(8,128)(2,1)S(1)}, bf16[1,1,64,32,256]{4,3,2,1,0:T(8,128)(2,1)}, u32[]{:S(2)}) copy-start(bf16[1,1,64,32,256]{4,3,2,1,0:T(8,128)(2,1)} %param.18) | copy-start | bytes 3145732
Sparse Core Ops, SparseCore 0:
  292.6 94.8 reduce-scatter.1
where the time goes:
time: 397 us; the launch traced here: 396 us
  matrix products  148 us (37%)
  waiting for transfers between devices  108 us (27%)
  blocking collectives  58.7 us (15%)
  local copies, waits for them, and re-layouts  53.6 us (14%)
  between operations  13.6 us (3%)
  other arithmetic  9.4 us (2%)
    dot_general x9, matrix products, cluster_total(): jnp.einsum('tn,njr->tjr', selector, terms, precision=lax.Precision.HIGHEST)  103 us
    reduce_scatter x1, waiting for transfers between devices, shards(): lax.psum_scatter(accumulated.reshape(clusters * LEAF, CASES), 'col', scat...  95 us
    all_to_all x1, blocking collectives, shards(): lax.all_to_all(right_sent, 'blk', split_axis=0, concat_axis=0, tiled=True)  58.7 us
    dot_general x8, matrix products, add_sender(): jnp.einsum('nki,nkr->nir', right_panels, coefficients, preferred_element_...  31.7 us
    dot_general x1, local copies, waits for them, and re-layouts, shards(): jnp.einsum('nij,nir->njr', dense_panels, dense_picked, preferred_element_...  17.1 us
    all_to_all x1, waiting for transfers between devices, shards(): lax.all_to_all(left_sent, 'blk', split_axis=0, concat_axis=0, tiled=True)  13.3 us
    dot_general x1, matrix products, shards(): jnp.einsum('nij,nir->njr', dense_panels, dense_picked, preferred_element_...  13.2 us
    while x32, local copies, waits for them, and re-layouts  10.3 us
  transfers between devices with their start and end apart: 2, of which 2 were waited for; matrix products, arithmetic and copies ran while one was open for 10% of the time, Pallas kernels for 0%

commit v1 on v0

v1 whole, which is shorter than its diff:
```python
import jax
import jax.numpy as jnp
from jax import lax
from jax.experimental import pallas as pl
from jax.experimental.pallas import tpu as pltpu
from jax.sharding import PartitionSpec as P

LEAF = 256
HALF = 128
CASES = 256
RANK = 32
SOURCES = 8
TARGETS = 32
DENSE = 60
LOW = 64
CAP = 16
PLANES = 8
NEAR = (1, 7, 2, 6)
FAR = (4, 3, 5)
MESH = pl.DeviceIdType.MESH
MIB = 1 << 20
BF16 = jnp.bfloat16
F32 = jnp.float32


def spec(space):
    return pl.BlockSpec(memory_space=space)


def place():
    b = lax.axis_index("blk")
    c = lax.axis_index("col")
    return b, lax.div(c, 8), lax.rem(lax.div(c, 2), 4), lax.rem(c, 2)


def contribution(pair):
    return lax.dot_general(
        pair[RANK:], pair[:RANK], (((0,), (0,)), ((), ())), preferred_element_type=F32
    )


def pack_kernel(
    owner, source, target, loads, left, right, slots, far, acc, stage, zero, count, where, seen, sem
):
    b = lax.axis_index("blk")
    zero[...] = jnp.zeros_like(zero)
    for d in range(PLANES):
        count[d] = 0

    @pl.loop(0, len(FAR) * TARGETS)
    def _(i):
        seen[i] = 0

    def one(n, carry):
        d = lax.rem(owner[b, n] - b + PLANES, PLANES)
        r = count[d]
        count[d] = r + 1
        where[d * CAP + r] = target[b, n]
        coefficients = jnp.dot(left[n], loads[source[b, n]], preferred_element_type=F32)
        slots[d, r, :RANK, :] = right[n]
        slots[d, r, RANK:, :] = coefficients.astype(BF16)
        return carry

    lax.fori_loop(0, LOW, one, 0, unroll=8)

    for e, d in enumerate(FAR):

        @pl.loop(0, count[d])
        def _(r):
            t = where[d * CAP + r]
            term = contribution(slots[d, r])
            first = seen[e * TARGETS + t] == 0

            @pl.when(first)
            def _():
                acc[t] = term
                seen[e * TARGETS + t] = 1

            @pl.when(jnp.logical_not(first))
            def _():
                acc[t] += term

        @pl.loop(0, TARGETS)
        def _(t):
            has = seen[e * TARGETS + t] == 1

            @pl.when(has)
            def _():
                stage[e, t] = acc[t].astype(BF16)
                pltpu.make_async_copy(stage.at[e, t], far.at[e, t], sem.at[e]).start()

            @pl.when(jnp.logical_not(has))
            def _():
                pltpu.make_async_copy(zero, far.at[e, t], sem.at[e]).start()

    for e in range(len(FAR)):
        pltpu.make_async_copy(stage.at[e], far.at[e], sem.at[e]).wait()


def pack(owner, source, target, loads, left, right):
    return pl.pallas_call(
        pack_kernel,
        out_shape=(
            jax.ShapeDtypeStruct((PLANES, CAP, 2 * RANK, LEAF), BF16),
            jax.ShapeDtypeStruct((len(FAR), TARGETS, CASES, LEAF), BF16),
        ),
        in_specs=[spec(pltpu.SMEM)] * 3 + [spec(pltpu.VMEM)] * 3,
        out_specs=(spec(pltpu.VMEM), spec(pl.ANY)),
        scratch_shapes=[
            pltpu.VMEM((TARGETS, CASES, LEAF), F32),
            pltpu.VMEM((len(FAR), TARGETS, CASES, LEAF), BF16),
            pltpu.VMEM((CASES, LEAF), BF16),
            pltpu.SMEM((PLANES,), jnp.int32),
            pltpu.SMEM((PLANES * CAP,), jnp.int32),
            pltpu.SMEM((len(FAR) * TARGETS,), jnp.int32),
            pltpu.SemaphoreType.DMA((len(FAR),)),
        ],
        compiler_params=pltpu.CompilerParams(vmem_limit_bytes=48 * MIB),
        name="pack",
    )(owner, source, target, loads, left, right)


def reduce_scratch(dtype):
    return [
        pltpu.VMEM((2, 4, 4, HALF, LEAF), dtype),
        pltpu.VMEM((2, 4, 4, HALF, LEAF), dtype),
        pltpu.VMEM((2, 3, 4, HALF, LEAF), BF16),
        pltpu.VMEM((2, 3, 4, HALF, LEAF), BF16),
        pltpu.VMEM((2, 3, HALF, LEAF), BF16),
        pltpu.VMEM((2, 3, HALF, LEAF), BF16),
        pltpu.VMEM((2, HALF, LEAF), F32),
        pltpu.SemaphoreType.DMA((2, 4, 3)),
        pltpu.SemaphoreType.DMA((2, 3, 4)),
    ]


ORDER = (2, 1, 3, 0)


class PlaneSum:
    def __init__(self, source, scratch):
        self.source = source
        (self.own, self.pair, self.s1, self.r1, self.s2, self.r2, self.kept, self.csem, self.nsem) = scratch
        self.b, self.y, self.x, self.k = place()
        self.sends = []

    def device(self, ax, d):
        y, x = self.y, self.x
        if ax == 0:
            x = lax.rem(x + d, 4)
        else:
            y = lax.rem(y + d, 4)
        return (self.b, (y * 4 + x) * 2 + self.k)

    def chunk(self, ax, d, core):
        if ax == 0:
            return self.source.at[:, lax.rem(self.x + d, 4), core, pl.ds(0, HALF), :]
        return self.source.at[lax.rem(self.y + d, 4), :, core, pl.ds(HALF, HALF), :]

    def local_copy(self, ax, d):
        return pltpu.make_async_copy(self.chunk(ax, d, self.k), self.own.at[ax, d], self.csem.at[ax, d, 0])

    def pair_copy(self, ax, d):
        return pltpu.make_async_remote_copy(
            src_ref=self.chunk(ax, d, 1 - self.k),
            dst_ref=self.pair.at[ax, d],
            send_sem=self.csem.at[ax, d, 1],
            recv_sem=self.csem.at[ax, d, 2],
            device_id=(self.b, (self.y * 4 + self.x) * 2 + 1 - self.k),
            device_id_type=MESH,
        )

    def begin(self):
        for d in ORDER:
            for ax in range(2):
                self.pair_copy(ax, d).start()
                self.local_copy(ax, d).start()

    def copy1(self, ax, d):
        return pltpu.make_async_remote_copy(
            src_ref=self.s1.at[ax, d - 1],
            dst_ref=self.r1.at[ax, d - 1],
            send_sem=self.nsem.at[ax, d - 1, 0],
            recv_sem=self.nsem.at[ax, d - 1, 1],
            device_id=self.device(ax, d),
            device_id_type=MESH,
        )

    def copy2(self, ax, d):
        return pltpu.make_async_remote_copy(
            src_ref=self.s2.at[ax, d - 1],
            dst_ref=self.r2.at[ax, d - 1],
            send_sem=self.nsem.at[ax, d - 1, 2],
            recv_sem=self.nsem.at[ax, d - 1, 3],
            device_id=self.device(1 - ax, d),
            device_id_type=MESH,
        )

    def arrived(self, ax, d):
        self.local_copy(ax, d).wait()
        self.pair_copy(ax, d).wait()

    def first(self):
        for d in ORDER[:3]:
            for ax in range(2):
                self.arrived(ax, d)

                @pl.loop(0, 4)
                def _(q):
                    total = self.own[ax, d, q].astype(F32) + self.pair[ax, d, q].astype(F32)
                    self.s1[ax, d - 1, q] = total.astype(BF16)

                self.copy1(ax, d).start()

    def second(self):
        for ax in range(2):
            self.arrived(ax, 0)
            for d in (1, 3, 2):
                self.copy1(ax, d).wait_recv()
            mine = self.y if ax == 0 else self.x
            for d in ORDER:
                q = lax.rem(mine + d, 4)
                total = self.own[ax, 0, q].astype(F32) + self.pair[ax, 0, q].astype(F32)
                for p in range(3):
                    total = total + self.r1[ax, p, q].astype(F32)
                if d == 0:
                    self.kept[ax] = total
                else:
                    self.s2[ax, d - 1] = total.astype(BF16)
                    self.copy2(ax, d).start()

    def total(self, ax):
        for d in (1, 3, 2):
            self.copy2(ax, d).wait_recv()
        total = self.kept[ax]
        for p in range(3):
            total = total + self.r2[ax, p].astype(F32)
        return total

    def finish(self):
        for ax in range(2):
            for d in range(1, 4):
                self.copy1(ax, d).wait_send()
                self.copy2(ax, d).wait_send()

    def partners(self):
        near = [self.device(ax, d) for ax in range(2) for d in range(1, 4)]
        return near + [(self.b, (self.y * 4 + self.x) * 2 + 1 - self.k)]


def greet(partners):
    barrier = pltpu.get_barrier_semaphore()
    for partner in partners:
        pl.semaphore_signal(barrier, inc=1, device_id=partner, device_id_type=MESH)
    pl.semaphore_wait(barrier, len(partners))


def exchange_kernel(slots, far, received, results, *scratch):
    sums = [PlaneSum(far.at[e], scratch[9 * e : 9 * e + 9]) for e in range(len(FAR))]
    zsem = scratch[-1]
    b = lax.axis_index("blk")
    c = lax.axis_index("col")

    def above(d):
        return (lax.rem(b + d, PLANES), c)

    greet(sums[0].partners() + [above(d) for d in NEAR])
    moves = [
        pltpu.make_async_remote_copy(
            src_ref=slots.at[d],
            dst_ref=received.at[i],
            send_sem=zsem.at[i, 0],
            recv_sem=zsem.at[i, 1],
            device_id=above(d),
            device_id_type=MESH,
        )
        for i, d in enumerate(NEAR)
    ]
    for move in moves:
        move.start()
    for s in sums:
        s.begin()
    sums[0].first()
    sums[1].first()
    sums[0].second()
    sums[2].first()
    sums[1].second()
    for e, s in enumerate(sums):
        if e == 2:
            s.second()
        for ax in range(2):
            results[e, ax * HALF : (ax + 1) * HALF, :] = s.total(ax).astype(BF16)
    for s in sums:
        s.finish()
    for move in moves:
        move.wait()


def exchange(slots, far):
    scratch = []
    for _ in FAR:
        scratch += reduce_scratch(BF16)
    return pl.pallas_call(
        exchange_kernel,
        out_shape=(
            jax.ShapeDtypeStruct((len(NEAR), CAP, 2 * RANK, LEAF), BF16),
            jax.ShapeDtypeStruct((len(FAR), CASES, LEAF), BF16),
        ),
        in_specs=[spec(pl.ANY)] * 2,
        out_specs=(spec(pl.ANY), spec(pltpu.VMEM)),
        scratch_shapes=scratch + [pltpu.SemaphoreType.DMA((len(NEAR), 2))],
        compiler_params=pltpu.CompilerParams(
            collective_id=1, has_side_effects=True, vmem_limit_bytes=48 * MIB
        ),
        name="exchange",
    )(slots, far)


def gather_kernel(
    owner, target, dsource, dtarget, loads, slots, received, dense, out,
    acc, turned, blocks, pairs, ids, spots, dsem, psem, osem,
):
    b = lax.axis_index("blk")
    pieces = 4
    part = DENSE // pieces
    pair_copies = [
        pltpu.make_async_copy(slots.at[0], pairs.at[pl.ds(0, CAP)], psem.at[0])
    ] + [
        pltpu.make_async_copy(received.at[i], pairs.at[pl.ds((i + 1) * CAP, CAP)], psem.at[i + 1])
        for i in range(len(NEAR))
    ]
    dense_copies = [
        pltpu.make_async_copy(dense.at[pl.ds(p * part, part)], blocks.at[pl.ds(p * part, part)], dsem.at[p])
        for p in range(pieces)
    ]
    for copy in pair_copies + dense_copies:
        copy.start()

    @pl.loop(0, TARGETS)
    def _(t):
        acc[t] = jnp.zeros((CASES, LEAF), F32)

    for s in range(SOURCES):
        turned[s] = loads[s].T

    length = jnp.int32(0)
    for i, d in enumerate((0,) + NEAR):
        sender = lax.rem(b - d + PLANES, PLANES)

        def scan(n, carry, i=i, sender=sender):
            length, rank = carry
            hit = owner[sender, n] == b
            ids[length] = target[sender, n]
            spots[length] = i * CAP + rank
            step = hit.astype(jnp.int32)
            return length + step, rank + step

        length, _ = lax.fori_loop(0, LOW, scan, (length, jnp.int32(0)), unroll=8)

    for copy in pair_copies:
        copy.wait()

    @pl.loop(0, length)
    def _(j):
        acc[ids[j]] += contribution(pairs[spots[j]])

    for p in range(pieces):
        dense_copies[p].wait()

        @pl.loop(p * part, (p + 1) * part)
        def _(n):
            acc[dtarget[n]] += jnp.dot(turned[dsource[n]], blocks[n], preferred_element_type=F32)

    whole = pltpu.make_async_copy(acc, out, osem)
    whole.start()
    whole.wait()


def gather(owner, target, dsource, dtarget, loads, slots, received, dense):
    return pl.pallas_call(
        gather_kernel,
        out_shape=jax.ShapeDtypeStruct((TARGETS, CASES, LEAF), F32),
        in_specs=[spec(pltpu.SMEM)] * 4 + [spec(pltpu.VMEM)] + [spec(pl.ANY)] * 3,
        out_specs=spec(pl.ANY),
        scratch_shapes=[
            pltpu.VMEM((TARGETS, CASES, LEAF), F32),
            pltpu.VMEM((SOURCES, CASES, LEAF), BF16),
            pltpu.VMEM((DENSE, LEAF, LEAF), BF16),
            pltpu.VMEM(((1 + len(NEAR)) * CAP, 2 * RANK, LEAF), BF16),
            pltpu.SMEM(((1 + len(NEAR)) * CAP + 1,), jnp.int32),
            pltpu.SMEM(((1 + len(NEAR)) * CAP + 1,), jnp.int32),
            pltpu.SemaphoreType.DMA((4,)),
            pltpu.SemaphoreType.DMA((1 + len(NEAR),)),
            pltpu.SemaphoreType.DMA,
        ],
        compiler_params=pltpu.CompilerParams(vmem_limit_bytes=48 * MIB),
        name="gather",
    )(owner, target, dsource, dtarget, loads, slots, received, dense)


def final_kernel(source, results, out, *scratch):
    own = PlaneSum(source, scratch[:9])
    landed, zsem = scratch[9:]
    b = lax.axis_index("blk")
    c = lax.axis_index("col")

    def above(d):
        return (lax.rem(b + d, PLANES), c)

    greet(own.partners() + [above(d) for d in FAR])
    moves = [
        pltpu.make_async_remote_copy(
            src_ref=results.at[e],
            dst_ref=landed.at[e],
            send_sem=zsem.at[e, 0],
            recv_sem=zsem.at[e, 1],
            device_id=above(d),
            device_id_type=MESH,
        )
        for e, d in enumerate(FAR)
    ]
    own.begin()
    for move in moves:
        move.start()
    own.first()
    own.second()
    for move in moves:
        move.wait()
    for ax in range(2):
        total = own.total(ax)
        for e in range(len(FAR)):
            total = total + landed[e, ax * HALF : (ax + 1) * HALF, :].astype(F32)
        out[:, ax * HALF : (ax + 1) * HALF] = total.T.astype(BF16)
    own.finish()


def final(source, results):
    return pl.pallas_call(
        final_kernel,
        out_shape=jax.ShapeDtypeStruct((LEAF, CASES), BF16),
        in_specs=[spec(pl.ANY)] * 2,
        out_specs=spec(pltpu.VMEM),
        scratch_shapes=reduce_scratch(F32)
        + [pltpu.VMEM((len(FAR), CASES, LEAF), BF16), pltpu.SemaphoreType.DMA((len(FAR), 2))],
        compiler_params=pltpu.CompilerParams(
            collective_id=2, has_side_effects=True, vmem_limit_bytes=48 * MIB
        ),
        name="final",
    )(source, results)


def shards(
    loads,
    dense_blocks,
    dense_source,
    dense_target,
    left_factors,
    right_factors,
    block_owner,
    block_source,
    block_target,
):
    loads = loads.reshape(SOURCES, LEAF, CASES)
    owner = block_owner.reshape(PLANES, LOW)
    source = block_source.reshape(PLANES, LOW)
    target = block_target.reshape(PLANES, LOW)
    left = left_factors.reshape(LOW, RANK, LEAF)
    right = right_factors.reshape(LOW, RANK, LEAF)
    slots, far = pack(owner, source, target, loads, left, right)
    received, results = exchange(slots, far.reshape(len(FAR), 4, 4, 2, CASES, LEAF))
    sums = gather(
        owner, target, dense_source.reshape(DENSE), dense_target.reshape(DENSE),
        loads, slots, received, dense_blocks.reshape(DENSE, LEAF, LEAF),
    )
    return final(sums.reshape(4, 4, 2, CASES, LEAF), results)


def solution(mesh):
    placed = (
        P("col", None),
        P("blk", "col", None, None, None),
        P("blk", "col", None),
        P("blk", "col", None),
        P("blk", "col", None, None, None),
        P("blk", "col", None, None, None),
        P(None, "col", None, None),
        P(None, "col", None),
        P(None, "col", None),
    )
    return jax.shard_map(
        shards, mesh=mesh, in_specs=placed, out_specs=P(("blk", "col"), None), check_vma=False
    )
```

time: 397 us -> 141 us (0.36)
  matrix products: 148 us -> 0 us
  Pallas kernels: 0 us -> 134 us
  waiting for transfers between devices: 108 us -> 0 us
  blocking collectives: 58.7 us -> 0 us
  local copies, waits for them, and re-layouts: 53.6 us -> 6.41 us
  between operations: 13.6 us -> 0.09 us
  other arithmetic: 9.4 us -> 0 us
    dot_general x18 -> x0, matrix products: 148 us -> none  [the longest x9 103 us: cluster_total(): jnp.einsum('tn,njr->tjr', selector, terms, precision=lax.Precision.HIGHEST)]
    pallas_call x0 -> x4, Pallas kernels: none -> 134 us  [the longest x1 59.1 us: exchange(): pl.pallas_call(exchange_kernel, out_shape=(jax.ShapeDtypeStruct((len(NEAR...]
    reduce_scatter x1 -> x0, waiting for transfers between devices: 95 us -> none  [shards(): lax.psum_scatter(accumulated.reshape(clusters * LEAF, CASES), 'col', scat...]
    all_to_all x1 -> x0, blocking collectives: 58.7 us -> none  [shards(): lax.all_to_all(right_sent, 'blk', split_axis=0, concat_axis=0, tiled=True)]
    dot_general x1 -> x0, local copies, waits for them, and re-layouts: 17.1 us -> none  [shards(): jnp.einsum('nij,nir->njr', dense_panels, dense_picked, preferred_element_...]
    gather x16 -> x0, local copies, waits for them, and re-layouts: 17 us -> none  [the longest x8 5.44 us: add_sender(): picked_rows = source_group[source_ids]]
    all_to_all x1 -> x0, waiting for transfers between devices: 13.3 us -> none  [shards(): lax.all_to_all(left_sent, 'blk', split_axis=0, concat_axis=0, tiled=True)]
    while x32 -> x0, local copies, waits for them, and re-layouts: 10.3 us -> none
  transfers between devices with their start and end apart: 2 -> 0, of which waited for: 2 -> 0; matrix products, arithmetic and copies ran while one was open for 10% -> 0% of each run, Pallas kernels for 0% -> 0%
where the time goes in v1:
time: 141 us
  Pallas kernels  134 us (95%)
  local copies, waits for them, and re-layouts  6.41 us (5%)
    pallas_call x1, Pallas kernels, exchange(): pl.pallas_call(exchange_kernel, out_shape=(jax.ShapeDtypeStruct((len(NEAR...  59.1 us
    pallas_call x1, Pallas kernels, final(): pl.pallas_call(final_kernel, out_shape=jax.ShapeDtypeStruct((LEAF, CASES)...  35.4 us
    pallas_call x1, Pallas kernels, gather(): pl.pallas_call(gather_kernel, out_shape=jax.ShapeDtypeStruct((TARGETS, CA...  23.4 us
    pallas_call x1, Pallas kernels, pack(): pl.pallas_call(pack_kernel, out_shape=(jax.ShapeDtypeStruct((PLANES, CAP,...  16.2 us
    unnamed x19, local copies, waits for them, and re-layouts  6.41 us

profile of v1, /device:TPU:1, one launch (start us, length us, event | category | flops | bytes accessed | tf_op | source)
XLA Modules:
  0.0 140.6 jit_solution(5295262920215665581)
XLA Ops:
  0.0 0.0 copy-start
  0.0 1.2 copy-done
  1.2 0.0 copy-start.2
  1.2 1.2 copy-done.2
  2.5 0.0 copy-start.3
  2.5 1.2 copy-done.3
  3.7 0.0 copy-start.4
  3.7 0.7 copy-done.4
  4.4 0.0 copy-start.5
  4.4 0.7 copy-done.5
  5.1 0.0 copy-start.6
  5.1 0.7 copy-done.6
  5.7 16.2 %pack.1 = (bf16[8,16,64,256]{3,2,1,0:T(8,128)(2,1)}, bf16[3,32,256,256]{3,2,1,0:T(8,128)(2,1)}) custom-call(s32[8,64]{1,0:T(8,128)S(1)} %bitcast.15, s32[8,64]{1,0:T(8,128)S(1)} %bitcast.19, s32[8,64]{1,0:T(8,128)S(1)} %bitcast.17, bf16[8,256,256]{2,1,0:T(8,128)(2,1)S(1)} %bitcast.11, bf16[64,32,256]{2,1,0:T(8,128)(2,1)S(1)} %bitcast.13, ...), custom_call_target="tpu_custom_call" | custom-call | tf_op jit(solution)/shard_map/pack/pallas_call | solution.py:101
  22.0 0.0 copy-start.1
  22.0 0.0 copy-start.7
  22.0 0.0 copy-start.8
  22.0 59.1 %exchange.1 = (bf16[4,16,64,256]{3,2,1,0:T(8,128)(2,1)S(1)}, bf16[3,256,256]{2,1,0:T(8,128)(2,1)S(1)}) custom-call(bf16[8,16,64,256]{3,2,1,0:T(8,128)(2,1)} %get-tuple-element.9.slots, bf16[3,4,4,2,256,256]{5,4,3,2,1,0:T(8,128)(2,1)} %bitcast.23), custom_call_target="tpu_custom_call" | custom-call | tf_op jit(solution)/shard_map/exchange/pallas_call | solution.py:303
  81.1 0.0 copy-done.1
  81.1 0.0 copy-done.7
  81.2 0.0 copy-done.8
  81.2 23.4 %gather.1 = f32[32,256,256]{2,1,0:T(8,128)} custom-call(s32[8,64]{1,0:T(8,128)S(1)} %bitcast.16, s32[8,64]{1,0:T(8,128)S(1)} %bitcast.18, s32[60]{0:T(128)S(1)} %bitcast.20, s32[60]{0:T(128)S(1)} %bitcast.21, bf16[8,256,256]{2,1,0:T(8,128)(2,1)S(1)} %bitcast.12, bf16[8,16,64,256]{3,2,1,0:T(8,128)(2,1)} %get-tuple-element.9.slots, ...), custom_call_target="tpu_custom_call" | custom-call | tf_op jit(solution)/shard_map/gather/pallas_call | solution.py:380
  104.6 35.4 %final.1 = bf16[256,256]{1,0:T(8,128)(2,1)S(1)} custom-call(f32[4,4,2,256,256]{4,3,2,1,0:T(8,128)} %bitcast.22, bf16[3,256,256]{2,1,0:T(8,128)(2,1)S(1)} %get-tuple-element.12.results), custom_call_target="tpu_custom_call" | custom-call | tf_op jit(solution)/shard_map/final/pallas_call | solution.py:438
  139.9 0.7 copy.11
Async XLA Ops:
  0.0 1.2 copy-start
  1.2 1.2 copy-start.2
  2.5 1.2 copy-start.3
  3.7 0.7 copy-start.4
  4.4 0.7 copy-start.5
  5.1 0.7 copy-start.6
  22.0 59.2 %copy-start.1 = (bf16[2048,256]{1,0:T(8,128)(2,1)S(1)}, bf16[2048,256]{1,0:T(8,128)(2,1)}, u32[]{:S(2)}) copy-start(bf16[2048,256]{1,0:T(8,128)(2,1)} %param.9) | copy-start | bytes 3145732
  22.0 59.2 %copy-start.7 = (s32[1,1,60]{2,1,0:T(1,128)S(1)}, s32[1,1,60]{2,1,0:T(1,128)}, u32[]{:S(2)}) copy-start(s32[1,1,60]{2,1,0:T(1,128)} %param.11) | copy-start | bytes 724
  22.0 59.2 %copy-start.8 = (s32[1,1,60]{2,1,0:T(1,128)S(1)}, s32[1,1,60]{2,1,0:T(1,128)}, u32[]{:S(2)}) copy-start(s32[1,1,60]{2,1,0:T(1,128)} %param.12) | copy-start | bytes 724

commit v2 on v1

v2 whole, which is shorter than its diff:
```python
import jax
import jax.numpy as jnp
from jax import lax
from jax.experimental import pallas as pl
from jax.experimental.pallas import tpu as pltpu
from jax.sharding import PartitionSpec as P

LEAF = 256
HALF = 128
CASES = 256
RANK = 32
SOURCES = 8
TARGETS = 32
DENSE = 60
LOW = 64
CAP = 16
PLANES = 8
GROUP = 4
PIECES = 4
ORDERED = 0
SOURCED = 64
TARGETED = 128
SAME = 192
LAST = 256
HAS = 288
IDS = 320
SPOTS = 416
LENGTH = 508
TABLE = 512
NULL = 80
NEAR = (1, 7, 2, 6)
FAR = (4, 3, 5)
MESH = pl.DeviceIdType.MESH
MIB = 1 << 20
BF16 = jnp.bfloat16
F32 = jnp.float32


def spec(space):
    return pl.BlockSpec(memory_space=space)


def place():
    b = lax.axis_index("blk")
    c = lax.axis_index("col")
    return b, lax.div(c, 8), lax.rem(lax.div(c, 2), 4), lax.rem(c, 2)


def contribution(pair):
    return lax.dot_general(
        pair[RANK:], pair[:RANK], (((0,), (0,)), ((), ())), preferred_element_type=F32
    )


def pack_kernel(
    owner_in, source_in, target_in, dsource_in, dtarget_in, loads_in, left_in, right_in, slots_out, far, tables,
    owner, source, target, dsource, dtarget, loads, left, right, slots, acc, stage, zero, count, where, seen,
    tsem, vsem, sem,
):
    b = lax.axis_index("blk")
    small = [
        pltpu.make_async_copy(x, y, tsem.at[i])
        for i, (x, y) in enumerate(
            (
                (owner_in, owner),
                (source_in, source),
                (target_in, target),
                (dsource_in, dsource),
                (dtarget_in, dtarget),
            )
        )
    ]
    large = [
        pltpu.make_async_copy(x, y, vsem.at[i])
        for i, (x, y) in enumerate(((loads_in, loads), (left_in, left), (right_in, right)))
    ]
    for copy in small + large:
        copy.start()
    zero[...] = jnp.zeros_like(zero)
    for d in range(PLANES):
        count[d] = 0
    for t in range(TARGETS):
        tables[HAS + t] = 0
        tables[LAST + t] = 0

    def clear(i, carry):
        seen[i] = 0
        return carry

    lax.fori_loop(0, len(FAR) * TARGETS, clear, 0, unroll=16)
    for copy in small:
        copy.wait()

    def tally(n, carry):
        t = dtarget[n]
        tables[HAS + t] = tables[HAS + t] + 1
        return carry

    lax.fori_loop(0, DENSE, tally, 0, unroll=4)
    start = jnp.int32(0)
    for t in range(TARGETS):
        tables[LAST + t] = start
        start = start + tables[HAS + t]

    def sort(n, carry):
        t = dtarget[n]
        spot = tables[LAST + t]
        tables[LAST + t] = spot + 1
        tables[ORDERED + spot] = n
        tables[SOURCED + spot] = dsource[n]
        tables[TARGETED + spot] = t
        return carry

    lax.fori_loop(0, DENSE, sort, 0, unroll=4)
    tables[SAME] = 0

    def link(s, carry):
        tables[SAME + s] = (tables[TARGETED + s] == tables[TARGETED + s - 1]).astype(jnp.int32)
        return carry

    lax.fori_loop(1, DENSE, link, 0, unroll=4)
    for t in range(TARGETS):
        tables[HAS + t] = jnp.minimum(tables[HAS + t], 1)

    length = jnp.int32(0)
    for i, d in enumerate(NEAR + (0,)):
        sender = lax.rem(b - d + PLANES, PLANES)

        def scan(n, carry, i=i, sender=sender):
            length, rank = carry
            tables[IDS + length] = target[sender, n]
            tables[SPOTS + length] = i * CAP + rank
            step = (owner[sender, n] == b).astype(jnp.int32)
            return length + step, rank + step

        length, _ = lax.fori_loop(0, LOW, scan, (length, jnp.int32(0)), unroll=8)
    for j in range(GROUP):
        tables[IDS + length + j] = 0
        tables[SPOTS + length + j] = NULL
    tables[LENGTH] = length

    for copy in large:
        copy.wait()

    def one(n, carry):
        d = lax.rem(owner[b, n] - b + PLANES, PLANES)
        r = count[d]
        count[d] = r + 1
        where[d * CAP + r] = target[b, n]
        coefficients = jnp.dot(left[n], loads[source[b, n]], preferred_element_type=F32)
        slots[d, r, :RANK, :] = right[n]
        slots[d, r, RANK:, :] = coefficients.astype(BF16)
        return carry

    lax.fori_loop(0, LOW, one, 0, unroll=8)
    whole = pltpu.make_async_copy(slots, slots_out, vsem.at[0])
    for d in FAR:
        amount = count[d]

        def blank(r, carry, d=d):
            slots[d, r] = jnp.zeros((2 * RANK, LEAF), BF16)
            where[d * CAP + r] = 0
            return carry

        lax.fori_loop(amount, lax.div(amount + GROUP - 1, GROUP) * GROUP, blank, 0)
    whole.start()

    for e, d in enumerate(FAR):

        @pl.loop(0, lax.div(count[d] + GROUP - 1, GROUP))
        def _(g):
            terms = [contribution(slots[d, g * GROUP + i]) for i in range(GROUP)]
            for i in range(GROUP):
                t = where[d * CAP + g * GROUP + i]
                first = seen[e * TARGETS + t] == 0
                seen[e * TARGETS + t] = 1
                acc[t] = jnp.where(first, terms[i], acc[t] + terms[i])

        @pl.loop(0, TARGETS)
        def _(t):
            has = seen[e * TARGETS + t] == 1

            @pl.when(has)
            def _():
                stage[e, t] = acc[t].astype(BF16)
                pltpu.make_async_copy(stage.at[e, t], far.at[e, t], sem.at[e]).start()

            @pl.when(jnp.logical_not(has))
            def _():
                pltpu.make_async_copy(zero, far.at[e, t], sem.at[e]).start()

    for e in range(len(FAR)):
        pltpu.make_async_copy(stage.at[e], far.at[e], sem.at[e]).wait()
    whole.wait()


def pack(owner, source, target, dsource, dtarget, loads, left, right):
    return pl.pallas_call(
        pack_kernel,
        out_shape=(
            jax.ShapeDtypeStruct((PLANES, CAP, 2 * RANK, LEAF), BF16),
            jax.ShapeDtypeStruct((len(FAR), TARGETS, CASES, LEAF), BF16),
            jax.ShapeDtypeStruct((TABLE,), jnp.int32),
        ),
        in_specs=[spec(pl.ANY)] * 8,
        out_specs=(spec(pl.ANY), spec(pl.ANY), spec(pltpu.SMEM)),
        scratch_shapes=[
            pltpu.SMEM((PLANES, LOW), jnp.int32),
            pltpu.SMEM((PLANES, LOW), jnp.int32),
            pltpu.SMEM((PLANES, LOW), jnp.int32),
            pltpu.SMEM((DENSE,), jnp.int32),
            pltpu.SMEM((DENSE,), jnp.int32),
            pltpu.VMEM((SOURCES, LEAF, CASES), BF16),
            pltpu.VMEM((LOW, RANK, LEAF), BF16),
            pltpu.VMEM((LOW, RANK, LEAF), BF16),
            pltpu.VMEM((PLANES, CAP, 2 * RANK, LEAF), BF16),
            pltpu.VMEM((TARGETS, CASES, LEAF), F32),
            pltpu.VMEM((len(FAR), TARGETS, CASES, LEAF), BF16),
            pltpu.VMEM((CASES, LEAF), BF16),
            pltpu.SMEM((PLANES,), jnp.int32),
            pltpu.SMEM((PLANES * CAP,), jnp.int32),
            pltpu.SMEM((len(FAR) * TARGETS,), jnp.int32),
            pltpu.SemaphoreType.DMA((5,)),
            pltpu.SemaphoreType.DMA((3,)),
            pltpu.SemaphoreType.DMA((len(FAR),)),
        ],
        compiler_params=pltpu.CompilerParams(vmem_limit_bytes=60 * MIB),
        name="pack",
    )(owner, source, target, dsource, dtarget, loads, left, right)


def reduce_scratch(dtype, local):
    return ([pltpu.VMEM((2, 4, 4, HALF, LEAF), dtype)] if local else []) + [
        pltpu.VMEM((2, 4, 4, HALF, LEAF), dtype),
        pltpu.VMEM((2, 4, HALF, LEAF), BF16),
        pltpu.VMEM((2, 2, 2, HALF, LEAF), BF16),
        pltpu.VMEM((2, 2, 4, HALF, LEAF), BF16),
        pltpu.VMEM((2, 2, 4, HALF, LEAF), BF16),
        pltpu.VMEM((2, 3, HALF, LEAF), BF16),
        pltpu.VMEM((2, 3, HALF, LEAF), BF16),
        pltpu.VMEM((2, HALF, LEAF), F32),
        pltpu.SemaphoreType.DMA((2, 4, 3)),
        pltpu.SemaphoreType.DMA((2, 2, 3, 2)),
        pltpu.SemaphoreType.DMA((2, 3, 2)),
    ]


ORDER = (2, 1, 3, 0)
SIDES = (1, 3)


class PlaneSum:
    def __init__(self, source, scratch, local):
        self.source = source
        self.own = scratch[0] if local else None
        (
            self.pair, self.across, self.passing, self.s1, self.r1, self.s2, self.r2, self.kept,
            self.csem, self.msem, self.nsem,
        ) = scratch[1:] if local else scratch
        self.b, self.y, self.x, self.k = place()

    def device(self, ax, d):
        y, x = self.y, self.x
        if ax == 0:
            x = lax.rem(x + d, 4)
        else:
            y = lax.rem(y + d, 4)
        return (self.b, (y * 4 + x) * 2 + self.k)

    def chunk(self, ax, d, core):
        rows = pl.ds(ax * HALF if self.own is not None else 0, HALF)
        if ax == 0:
            return self.source[ax].at[:, lax.rem(self.x + d, 4), core, rows, :]
        return self.source[ax].at[lax.rem(self.y + d, 4), :, core, rows, :]

    def local_copy(self, ax, d):
        return pltpu.make_async_copy(self.chunk(ax, d, self.k), self.own.at[ax, d], self.csem.at[ax, d, 0])

    def pair_copy(self, ax, d):
        return pltpu.make_async_remote_copy(
            src_ref=self.chunk(ax, d, 1 - self.k),
            dst_ref=self.pair.at[ax, d],
            send_sem=self.csem.at[ax, d, 1],
            recv_sem=self.csem.at[ax, d, 2],
            device_id=(self.b, (self.y * 4 + self.x) * 2 + 1 - self.k),
            device_id_type=MESH,
        )

    def begin(self):
        for d in ORDER:
            for ax in range(2):
                self.pair_copy(ax, d).start()
                if self.own is not None:
                    self.local_copy(ax, d).start()

    def arrived(self, ax, d):
        if self.own is not None:
            self.local_copy(ax, d).wait()
        self.pair_copy(ax, d).wait()

    def mine(self, ax, d, q):
        if self.own is not None:
            value = self.own[ax, d, q]
        elif ax == 0:
            value = self.source[ax][q, lax.rem(self.x + d, 4), self.k]
        else:
            value = self.source[ax][lax.rem(self.y + d, 4), q, self.k]
        return value.astype(F32) + self.pair[ax, d, q].astype(F32)

    def ring_copy(self, ax, side, part):
        low = 2 * side if part == 0 else 2 * side if part == 2 else 2 - 2 * side
        rows = pl.ds(low, 2)
        return pltpu.make_async_remote_copy(
            src_ref=self.across.at[ax, rows] if part == 0 else self.s1.at[ax, side, rows],
            dst_ref=self.passing.at[ax, side] if part == 0 else self.r1.at[ax, side, rows],
            send_sem=self.msem.at[ax, side, part, 0],
            recv_sem=self.msem.at[ax, side, part, 1],
            device_id=self.device(ax, SIDES[side]),
            device_id_type=MESH,
        )

    def last_copy(self, ax, d):
        return pltpu.make_async_remote_copy(
            src_ref=self.s2.at[ax, d - 1],
            dst_ref=self.r2.at[ax, d - 1],
            send_sem=self.nsem.at[ax, d - 1, 0],
            recv_sem=self.nsem.at[ax, d - 1, 1],
            device_id=self.device(1 - ax, d),
            device_id_type=MESH,
        )

    def opposite(self):
        for ax in range(2):
            self.arrived(ax, 2)
            for side in range(2):

                @pl.loop(2 * side, 2 * side + 2)
                def _(q):
                    self.across[ax, q] = self.mine(ax, 2, q).astype(BF16)

                self.ring_copy(ax, side, 0).start()

    def beside(self):
        for side in range(2):
            for ax in range(2):
                self.arrived(ax, SIDES[side])

                @pl.loop(2 - 2 * side, 4 - 2 * side)
                def _(q):
                    self.s1[ax, side, q] = self.mine(ax, SIDES[side], q).astype(BF16)

                self.ring_copy(ax, side, 1).start()

    def relay(self):
        for ax in range(2):
            for side in range(2):
                self.ring_copy(ax, side, 0).wait_recv()

                @pl.loop(0, 2)
                def _(p):
                    q = 2 * side + p
                    total = self.mine(ax, SIDES[side], q) + self.passing[ax, side, p].astype(F32)
                    self.s1[ax, side, q] = total.astype(BF16)

                self.ring_copy(ax, side, 2).start()

    def turn(self):
        for ax in range(2):
            self.arrived(ax, 0)
        for ax in range(2):
            for part in (1, 2):
                for side in range(2):
                    self.ring_copy(ax, side, part).wait_recv()
            here = self.y if ax == 0 else self.x
            for d in ORDER:
                q = lax.rem(here + d, 4)
                total = self.mine(ax, 0, q)
                for side in range(2):
                    total = total + self.r1[ax, side, q].astype(F32)
                if d == 0:
                    self.kept[ax] = total
                else:
                    self.s2[ax, d - 1] = total.astype(BF16)
                    self.last_copy(ax, d).start()

    def total(self, ax):
        for d in (1, 3, 2):
            self.last_copy(ax, d).wait_recv()
        total = self.kept[ax]
        for p in range(3):
            total = total + self.r2[ax, p].astype(F32)
        return total

    def finish(self):
        for ax in range(2):
            for side in range(2):
                for part in range(3):
                    self.ring_copy(ax, side, part).wait_send()
            for d in range(1, 4):
                self.last_copy(ax, d).wait_send()

    def partners(self):
        near = [self.device(ax, d) for ax in range(2) for d in range(1, 4)]
        return near + [(self.b, (self.y * 4 + self.x) * 2 + 1 - self.k)]


def greet(partners):
    barrier = pltpu.get_barrier_semaphore()
    for partner in partners:
        pl.semaphore_signal(barrier, inc=1, device_id=partner, device_id_type=MESH)
    pl.semaphore_wait(barrier, len(partners))


def exchange_kernel(slots, far, tables_in, loads_in, dense, received, results, sums0, sums1, *scratch):
    sums = (sums0, sums1)
    planes = [PlaneSum((far.at[e], far.at[e]), scratch[12 * e : 12 * e + 12], True) for e in range(len(FAR))]
    tables, loads, turned, blocks, running, zsem, lsem, dsem = scratch[36:]
    b = lax.axis_index("blk")
    c = lax.axis_index("col")

    def above(d):
        return (lax.rem(b + d, PLANES), c)

    own_slots = pltpu.make_async_copy(slots.at[0], received.at[pl.ds(len(NEAR) * CAP, CAP)], lsem.at[0])
    table_copy = pltpu.make_async_copy(tables_in, tables, lsem.at[1])
    load_copy = pltpu.make_async_copy(loads_in, loads, lsem.at[2])
    part = DENSE // PIECES
    dense_copies = [
        pltpu.make_async_copy(dense.at[pl.ds(p * part, part)], blocks.at[pl.ds(p * part, part)], dsem.at[p])
        for p in range(PIECES)
    ]
    greet(planes[0].partners() + [above(d) for d in NEAR])
    moves = [
        pltpu.make_async_remote_copy(
            src_ref=slots.at[d],
            dst_ref=received.at[pl.ds(i * CAP, CAP)],
            send_sem=zsem.at[i, 0],
            recv_sem=zsem.at[i, 1],
            device_id=above(d),
            device_id_type=MESH,
        )
        for i, d in enumerate(NEAR)
    ]
    for plane in planes[:1]:
        plane.begin()
    for move in moves:
        move.start()
    for plane in planes[1:]:
        plane.begin()
    for copy in [table_copy, load_copy, own_slots] + dense_copies:
        copy.start()
    received[NULL] = jnp.zeros((2 * RANK, LEAF), BF16)

    def dense_sums(half):
        running[0] = jnp.zeros((HALF, LEAF), F32)

        @pl.loop(0, DENSE // GROUP)
        def _(g):
            terms = [
                jnp.dot(
                    turned[tables[SOURCED + g * GROUP + i], half * HALF : (half + 1) * HALF, :],
                    blocks[tables[ORDERED + g * GROUP + i]],
                    preferred_element_type=F32,
                )
                for i in range(GROUP)
            ]
            total = running[g * GROUP]
            for i in range(GROUP):
                total = total * tables[SAME + g * GROUP + i].astype(F32) + terms[i]
                running[g * GROUP + i + 1] = total

        @pl.loop(0, TARGETS)
        def _(t):
            sums[half][t] = running[tables[LAST + t]] * tables[HAS + t].astype(F32)


    planes[0].opposite()
    planes[0].beside()
    planes[1].opposite()
    planes[1].beside()
    planes[0].relay()
    planes[2].opposite()
    planes[2].beside()
    load_copy.wait()
    table_copy.wait()
    for s in range(SOURCES):
        turned[s] = loads[s].T
    planes[1].relay()
    for copy in dense_copies:
        copy.wait()
    dense_sums(0)
    planes[0].turn()
    planes[2].relay()
    dense_sums(1)
    planes[1].turn()
    planes[2].turn()
    for e, plane in enumerate(planes):
        for ax in range(2):
            results[e, ax * HALF : (ax + 1) * HALF, :] = plane.total(ax).astype(BF16)
    for plane in planes:
        plane.finish()
    own_slots.wait()
    for move in moves:
        move.wait()


def exchange(slots, far, tables, loads, dense):
    scratch = []
    for _ in FAR:
        scratch += reduce_scratch(BF16, True)
    return pl.pallas_call(
        exchange_kernel,
        out_shape=(
            jax.ShapeDtypeStruct((NULL + 1, 2 * RANK, LEAF), BF16),
            jax.ShapeDtypeStruct((len(FAR), CASES, LEAF), BF16),
            jax.ShapeDtypeStruct((TARGETS, HALF, LEAF), F32),
            jax.ShapeDtypeStruct((TARGETS, HALF, LEAF), F32),
        ),
        in_specs=[spec(pl.ANY)] * 5,
        out_specs=(spec(pltpu.VMEM),) * 4,
        scratch_shapes=scratch
        + [
            pltpu.SMEM((TABLE,), jnp.int32),
            pltpu.VMEM((SOURCES, LEAF, CASES), BF16),
            pltpu.VMEM((SOURCES, CASES, LEAF), BF16),
            pltpu.VMEM((DENSE, LEAF, LEAF), BF16),
            pltpu.VMEM((DENSE + 1, HALF, LEAF), F32),
            pltpu.SemaphoreType.DMA((len(NEAR), 2)),
            pltpu.SemaphoreType.DMA((5,)),
            pltpu.SemaphoreType.DMA((PIECES,)),
        ],
        compiler_params=pltpu.CompilerParams(
            collective_id=1, has_side_effects=True, vmem_limit_bytes=42 * MIB
        ),
        name="exchange",
    )(slots, far, tables, loads, dense)


def gather_kernel(tables, received, in0, in1, sums0, sums1):
    @pl.loop(0, lax.div(tables[LENGTH] + GROUP - 1, GROUP))
    def _(g):
        terms = [contribution(received[tables[SPOTS + g * GROUP + i]]) for i in range(GROUP)]
        for i in range(GROUP):
            t = tables[IDS + g * GROUP + i]
            sums0[t] += terms[i][:HALF]
            sums1[t] += terms[i][HALF:]


def gather(tables, received, sums):
    return pl.pallas_call(
        gather_kernel,
        out_shape=(jax.ShapeDtypeStruct((TARGETS, HALF, LEAF), F32),) * 2,
        in_specs=[spec(pltpu.SMEM)] + [spec(pltpu.VMEM)] * 3,
        out_specs=(spec(pltpu.VMEM),) * 2,
        input_output_aliases={2: 0, 3: 1},
        compiler_params=pltpu.CompilerParams(vmem_limit_bytes=8 * MIB),
        name="gather",
    )(tables, received, *sums)


def final_kernel(source0, source1, results, out, *scratch):
    own = PlaneSum((source0, source1), scratch[:11], False)
    landed, zsem = scratch[11:]
    b = lax.axis_index("blk")
    c = lax.axis_index("col")

    def above(d):
        return (lax.rem(b + d, PLANES), c)

    greet(own.partners() + [above(d) for d in FAR])
    moves = [
        pltpu.make_async_remote_copy(
            src_ref=results.at[e],
            dst_ref=landed.at[e],
            send_sem=zsem.at[e, 0],
            recv_sem=zsem.at[e, 1],
            device_id=above(d),
            device_id_type=MESH,
        )
        for e, d in enumerate(FAR)
    ]
    own.begin()
    for move in moves:
        move.start()
    own.opposite()
    own.beside()
    own.relay()
    own.turn()
    for move in moves:
        move.wait()
    for ax in range(2):
        total = own.total(ax)
        for e in range(len(FAR)):
            total = total + landed[e, ax * HALF : (ax + 1) * HALF, :].astype(F32)
        out[:, ax * HALF : (ax + 1) * HALF] = total.T.astype(BF16)
    own.finish()


def final(sums, results):
    return pl.pallas_call(
        final_kernel,
        out_shape=jax.ShapeDtypeStruct((LEAF, CASES), BF16),
        in_specs=[spec(pltpu.VMEM)] * 3,
        out_specs=spec(pltpu.VMEM),
        scratch_shapes=reduce_scratch(F32, False)
        + [pltpu.VMEM((len(FAR), CASES, LEAF), BF16), pltpu.SemaphoreType.DMA((len(FAR), 2))],
        compiler_params=pltpu.CompilerParams(
            collective_id=2, has_side_effects=True, vmem_limit_bytes=16 * MIB
        ),
        name="final",
    )(*[x.reshape(4, 4, 2, HALF, LEAF) for x in sums], results)


def shards(
    loads,
    dense_blocks,
    dense_source,
    dense_target,
    left_factors,
    right_factors,
    block_owner,
    block_source,
    block_target,
):
    loads = loads.reshape(SOURCES, LEAF, CASES)
    owner = block_owner.reshape(PLANES, LOW)
    source = block_source.reshape(PLANES, LOW)
    target = block_target.reshape(PLANES, LOW)
    left = left_factors.reshape(LOW, RANK, LEAF)
    right = right_factors.reshape(LOW, RANK, LEAF)
    slots, far, tables = pack(
        owner, source, target, dense_source.reshape(DENSE), dense_target.reshape(DENSE), loads, left, right
    )
    received, results, *sums = exchange(
        slots, far.reshape(len(FAR), 4, 4, 2, CASES, LEAF), tables, loads, dense_blocks.reshape(DENSE, LEAF, LEAF)
    )
    sums = gather(tables, received, sums)
    return final(sums, results)


def solution(mesh):
    placed = (
        P("col", None),
        P("blk", "col", None, None, None),
        P("blk", "col", None),
        P("blk", "col", None),
        P("blk", "col", None, None, None),
        P("blk", "col", None, None, None),
        P(None, "col", None, None),
        P(None, "col", None),
        P(None, "col", None),
    )
    return jax.shard_map(
        shards, mesh=mesh, in_specs=placed, out_specs=P(("blk", "col"), None), check_vma=False
    )
```

time: 141 us -> 92.7 us (0.66)
  Pallas kernels: 134 us -> 90 us
  local copies, waits for them, and re-layouts: 6.41 us -> 2.56 us
    pallas_call x2, Pallas kernels: 82.5 us -> 54.1 us  [the longest x1 48.5 us: exchange(): pl.pallas_call(exchange_kernel, out_shape=(jax.ShapeDtypeStruct((NULL + 1...]
    pallas_call x1, Pallas kernels: 35.4 us -> 23.2 us  [final(): pl.pallas_call(final_kernel, out_shape=jax.ShapeDtypeStruct((LEAF, CASES)...]
    unnamed x19 -> x5, local copies, waits for them, and re-layouts: 6.41 us -> 2.56 us
    pallas_call x1, Pallas kernels: 16.2 us -> 12.7 us  [pack(): pl.pallas_call(pack_kernel, out_shape=(jax.ShapeDtypeStruct((PLANES, CAP,...]
where the time goes in v2:
time: 92.7 us; the launch traced here: 92.6 us
  Pallas kernels  90 us (97%)
  local copies, waits for them, and re-layouts  2.56 us (3%)
    pallas_call x1, Pallas kernels, exchange(): pl.pallas_call(exchange_kernel, out_shape=(jax.ShapeDtypeStruct((NULL + 1...  48.5 us
    pallas_call x1, Pallas kernels, final(): pl.pallas_call(final_kernel, out_shape=jax.ShapeDtypeStruct((LEAF, CASES)...  23.2 us
    pallas_call x1, Pallas kernels, pack(): pl.pallas_call(pack_kernel, out_shape=(jax.ShapeDtypeStruct((PLANES, CAP,...  12.7 us
    pallas_call x1, Pallas kernels, gather(): pl.pallas_call(gather_kernel, out_shape=(jax.ShapeDtypeStruct((TARGETS, H...  5.63 us
    unnamed x5, local copies, waits for them, and re-layouts  2.56 us

profile of v2, /device:TPU:1, one launch (start us, length us, event | category | flops | bytes accessed | tf_op | source)
XLA Modules:
  0.0 92.6 jit_solution(9517381940997821127)
XLA Ops:
  0.0 12.7 %pack.1 = (bf16[8,16,64,256]{3,2,1,0:T(8,128)(2,1)}, bf16[3,32,256,256]{3,2,1,0:T(8,128)(2,1)}, s32[512]{0:T(512)}) custom-call(s32[8,64]{1,0:T(8,128)} %bitcast.20, s32[8,64]{1,0:T(8,128)} %bitcast.21, s32[8,64]{1,0:T(8,128)} %bitcast.22, s32[60]{0:T(128)} %bitcast.23, s32[60]{0:T(128)} %bitcast.24, bf16[8,256,256]{2,1,0:T(8,128)(2,1)} %bitcast.14, ...), custom_call_target="tpu_custom_call" | custom-call | tf_op jit(solution)/shard_map/pack/pallas_call | solution.py:198
  12.7 0.0 copy-start
  12.7 1.2 %copy-done = bf16[2048,256]{1,0:T(8,128)(2,1)S(1)} copy-done((bf16[2048,256]{1,0:T(8,128)(2,1)S(1)}, bf16[2048,256]{1,0:T(8,128)(2,1)}, u32[]{:S(2)}) %copy-start) | copy-done | bytes 1048600
  13.9 0.0 copy-start.1
  13.9 0.7 copy-done.1
  14.6 48.5 %exchange.1 = (bf16[81,64,256]{2,1,0:T(8,128)(2,1)S(1)}, bf16[3,256,256]{2,1,0:T(8,128)(2,1)S(1)}, f32[32,128,256]{2,1,0:T(8,128)S(1)}, f32[32,128,256]{2,1,0:T(8,128)S(1)}) custom-call(bf16[8,16,64,256]{3,2,1,0:T(8,128)(2,1)} %get-tuple-element.15.slots, bf16[3,4,4,2,256,256]{5,4,3,2,1,0:T(8,128)(2,1)} %bitcast.16, s32[512]{0:T(512)S(1)} %copy-done.1, ...), custom_call_target="tpu_custom_call" | custom-call | tf_op jit(solution)/shard_map/exchange/pallas_call | solution.py:511
  63.1 5.6 %gather.1 = (f32[32,128,256]{2,1,0:T(8,128)S(1)}, f32[32,128,256]{2,1,0:T(8,128)S(1)}) custom-call(s32[512]{0:T(512)S(1)} %copy-done.1, bf16[81,64,256]{2,1,0:T(8,128)(2,1)S(1)} %get-tuple-element.17.received, f32[32,128,256]{2,1,0:T(8,128)S(1)} %get-tuple-element.18.in0, ...), custom_call_target="tpu_custom_call", output_to_operand_aliasing={{0}: (2, {}), {1}: (3, {})} | custom-call | tf_op jit(solution)/shard_map/gather/pallas_call | solution.py:550
  68.7 23.2 %final.1 = bf16[256,256]{1,0:T(8,128)(2,1)S(1)} custom-call(f32[4,4,2,128,256]{4,3,2,1,0:T(8,128)S(1)} %bitcast.12, f32[4,4,2,128,256]{4,3,2,1,0:T(8,128)S(1)} %bitcast.13, bf16[3,256,256]{2,1,0:T(8,128)(2,1)S(1)} %get-tuple-element.22.results), custom_call_target="tpu_custom_call" | custom-call | tf_op jit(solution)/shard_map/final/pallas_call | solution.py:600
  91.9 0.7 copy.15
Async XLA Ops:
  12.7 1.2 %copy-start = (bf16[2048,256]{1,0:T(8,128)(2,1)S(1)}, bf16[2048,256]{1,0:T(8,128)(2,1)}, u32[]{:S(2)}) copy-start(bf16[2048,256]{1,0:T(8,128)(2,1)} %param.9) | copy-start | bytes 3145732
  13.9 0.7 copy-start.1

commit v3 on v2

--- a/solution.py
+++ b/solution.py
@@ -7,6 +7,7 @@
 
 LEAF = 256
 HALF = 128
+QUARTER = 64
 CASES = 256
 RANK = 32
 SOURCES = 8
@@ -20,13 +21,15 @@
 ORDERED = 0
 SOURCED = 64
 TARGETED = 128
-SAME = 192
 LAST = 256
 HAS = 288
 IDS = 320
 SPOTS = 416
 LENGTH = 508
-TABLE = 512
+FAR_ORDER = 512
+FAR_TARGET = 560
+FAR_LAST = 608
+TABLE = 768
 NULL = 80
 NEAR = (1, 7, 2, 6)
 FAR = (4, 3, 5)
@@ -53,9 +56,8 @@
 
 
 def pack_kernel(
-    owner_in, source_in, target_in, dsource_in, dtarget_in, loads_in, left_in, right_in, slots_out, far, tables,
-    owner, source, target, dsource, dtarget, loads, left, right, slots, acc, stage, zero, count, where, seen,
-    tsem, vsem, sem,
+    owner_in, source_in, target_in, dsource_in, dtarget_in, loads_in, left_in, right_in, slots_out, tables,
+    owner, source, target, dsource, dtarget, loads, left, right, slots, count, where, tsem, vsem,
 ):
     b = lax.axis_index("blk")
     small = [
@@ -76,7 +78,6 @@
     ]
     for copy in small + large:
         copy.start()
-    zero[...] = jnp.zeros_like(zero)
     for d in range(PLANES):
         count[d] = 0
     for t in range(TARGETS):
@@ -84,10 +85,17 @@
         tables[LAST + t] = 0
 
     def clear(i, carry):
-        seen[i] = 0
+        tables[FAR_LAST + i] = 0
         return carry
 
     lax.fori_loop(0, len(FAR) * TARGETS, clear, 0, unroll=16)
+
+    def blank(i, carry):
+        tables[FAR_ORDER + i] = 0
+        tables[FAR_TARGET + i] = 0
+        return carry
+
+    lax.fori_loop(0, len(FAR) * CAP, blank, 0, unroll=16)
     for copy in small:
         copy.wait()
 
@@ -112,13 +120,6 @@
         return carry
 
     lax.fori_loop(0, DENSE, sort, 0, unroll=4)
-    tables[SAME] = 0
-
-    def link(s, carry):
-        tables[SAME + s] = (tables[TARGETED + s] == tables[TARGETED + s - 1]).astype(jnp.int32)
-        return carry
-
-    lax.fori_loop(1, DENSE, link, 0, unroll=4)
     for t in range(TARGETS):
         tables[HAS + t] = jnp.minimum(tables[HAS + t], 1)
 
@@ -154,43 +155,42 @@
 
     lax.fori_loop(0, LOW, one, 0, unroll=8)
     whole = pltpu.make_async_copy(slots, slots_out, vsem.at[0])
-    for d in FAR:
+    whole.start()
+
+    for e, d in enumerate(FAR):
         amount = count[d]
 
-        def blank(r, carry, d=d):
-            slots[d, r] = jnp.zeros((2 * RANK, LEAF), BF16)
-            where[d * CAP + r] = 0
+        def add(r, carry, e=e, d=d):
+            t = where[d * CAP + r]
+            tables[FAR_LAST + e * TARGETS + t] = tables[FAR_LAST + e * TARGETS + t] + 1
             return carry
 
-        lax.fori_loop(amount, lax.div(amount + GROUP - 1, GROUP) * GROUP, blank, 0)
-    whole.start()
-
-    for e, d in enumerate(FAR):
-
-        @pl.loop(0, lax.div(count[d] + GROUP - 1, GROUP))
-        def _(g):
-            terms = [contribution(slots[d, g * GROUP + i]) for i in range(GROUP)]
-            for i in range(GROUP):
-                t = where[d * CAP + g * GROUP + i]
-                first = seen[e * TARGETS + t] == 0
-                seen[e * TARGETS + t] = 1
-                acc[t] = jnp.where(first, terms[i], acc[t] + terms[i])
-
-        @pl.loop(0, TARGETS)
-        def _(t):
-            has = seen[e * TARGETS + t] == 1
-
-            @pl.when(has)
-            def _():
-                stage[e, t] = acc[t].astype(BF16)
-                pltpu.make_async_copy(stage.at[e, t], far.at[e, t], sem.at[e]).start()
-
-            @pl.when(jnp.logical_not(has))
-            def _():
-                pltpu.make_async_copy(zero, far.at[e, t], sem.at[e]).start()
-
-    for e in range(len(FAR)):
-        pltpu.make_async_copy(stage.at[e], far.at[e], sem.at[e]).wait()
+        lax.fori_loop(0, amount, add, 0)
+
+        def begin(t, start, e=e):
+            held = tables[FAR_LAST + e * TARGETS + t]
+            tables[FAR_LAST + e * TARGETS + t] = start
+            return start + held
+
+        lax.fori_loop(0, TARGETS, begin, jnp.int32(0), unroll=8)
+
+        def put(r, carry, e=e, d=d):
+            t = where[d * CAP + r]
+            spot = tables[FAR_LAST + e * TARGETS + t]
+            tables[FAR_LAST + e * TARGETS + t] = spot + 1
+            tables[FAR_ORDER + e * CAP + spot] = r
+            tables[FAR_TARGET + e * CAP + spot] = t
+            return carry
+
+        lax.fori_loop(0, amount, put, 0)
+
+        def last(t, before, e=e):
+            end = tables[FAR_LAST + e * TARGETS + t]
+            tables[FAR_LAST + e * TARGETS + t] = jnp.where(end == before, 0, end)
+            return end
+
+        lax.fori_loop(0, TARGETS, last, jnp.int32(0), unroll=8)
+
     whole.wait()
 
 
@@ -199,11 +199,10 @@
         pack_kernel,
         out_shape=(
             jax.ShapeDtypeStruct((PLANES, CAP, 2 * RANK, LEAF), BF16),
-            jax.ShapeDtypeStruct((len(FAR), TARGETS, CASES, LEAF), BF16),
             jax.ShapeDtypeStruct((TABLE,), jnp.int32),
         ),
         in_specs=[spec(pl.ANY)] * 8,
-        out_specs=(spec(pl.ANY), spec(pl.ANY), spec(pltpu.SMEM)),
+        out_specs=(spec(pl.ANY), spec(pltpu.SMEM)),
         scratch_shapes=[
             pltpu.SMEM((PLANES, LOW), jnp.int32),
             pltpu.SMEM((PLANES, LOW), jnp.int32),
@@ -214,15 +213,10 @@
             pltpu.VMEM((LOW, RANK, LEAF), BF16),
             pltpu.VMEM((LOW, RANK, LEAF), BF16),
             pltpu.VMEM((PLANES, CAP, 2 * RANK, LEAF), BF16),
-            pltpu.VMEM((TARGETS, CASES, LEAF), F32),
-            pltpu.VMEM((len(FAR), TARGETS, CASES, LEAF), BF16),
-            pltpu.VMEM((CASES, LEAF), BF16),
             pltpu.SMEM((PLANES,), jnp.int32),
             pltpu.SMEM((PLANES * CAP,), jnp.int32),
-            pltpu.SMEM((len(FAR) * TARGETS,), jnp.int32),
             pltpu.SemaphoreType.DMA((5,)),
             pltpu.SemaphoreType.DMA((3,)),
-            pltpu.SemaphoreType.DMA((len(FAR),)),
         ],
         compiler_params=pltpu.CompilerParams(vmem_limit_bytes=60 * MIB),
         name="pack",
@@ -230,11 +224,9 @@
 
 
 def reduce_scratch(dtype, local):
-    return ([pltpu.VMEM((2, 4, 4, HALF, LEAF), dtype)] if local else []) + [
+    return [pltpu.VMEM((2, 4 if local else 3, 4, HALF, LEAF), BF16)] + [
         pltpu.VMEM((2, 4, 4, HALF, LEAF), dtype),
-        pltpu.VMEM((2, 4, HALF, LEAF), BF16),
         pltpu.VMEM((2, 2, 2, HALF, LEAF), BF16),
-        pltpu.VMEM((2, 2, 4, HALF, LEAF), BF16),
         pltpu.VMEM((2, 2, 4, HALF, LEAF), BF16),
         pltpu.VMEM((2, 3, HALF, LEAF), BF16),
         pltpu.VMEM((2, 3, HALF, LEAF), BF16),
@@ -250,13 +242,17 @@
 
 
 class PlaneSum:
-    def __init__(self, source, scratch, local):
+    def __init__(self, source, scratch, give):
+        local = give is not None
         self.source = source
+        self.give = give
+        self.given = False
         self.own = scratch[0] if local else None
+        self.sent = scratch[0]
         (
-            self.pair, self.across, self.passing, self.s1, self.r1, self.s2, self.r2, self.kept,
+            self.pair, self.passing, self.r1, self.s2, self.r2, self.kept,
             self.csem, self.msem, self.nsem,
-        ) = scratch[1:] if local else scratch
+        ) = scratch[1:]
         self.b, self.y, self.x, self.k = place()
 
     def device(self, ax, d):
@@ -268,13 +264,11 @@
         return (self.b, (y * 4 + x) * 2 + self.k)
 
     def chunk(self, ax, d, core):
-        rows = pl.ds(ax * HALF if self.own is not None else 0, HALF)
+        if self.give is not None:
+            return self.give.at[ax, d]
         if ax == 0:
-            return self.source[ax].at[:, lax.rem(self.x + d, 4), core, rows, :]
-        return self.source[ax].at[lax.rem(self.y + d, 4), :, core, rows, :]
-
-    def local_copy(self, ax, d):
-        return pltpu.make_async_copy(self.chunk(ax, d, self.k), self.own.at[ax, d], self.csem.at[ax, d, 0])
+            return self.source[ax].at[:, lax.rem(self.x + d, 4), core]
+        return self.source[ax].at[lax.rem(self.y + d, 4), :, core]
 
     def pair_copy(self, ax, d):
         return pltpu.make_async_remote_copy(
@@ -290,13 +284,49 @@
         for d in ORDER:
             for ax in range(2):
                 self.pair_copy(ax, d).start()
-                if self.own is not None:
-                    self.local_copy(ax, d).start()
+
+    def form(self, tables, e, slots, running):
+        for h in range(4):
+            running[h] = jnp.zeros((QUARTER, LEAF), F32)
+
+        @pl.loop(0, CAP // GROUP)
+        def _(g):
+            terms = [contribution(slots[tables[FAR_ORDER + e * CAP + g * GROUP + i]]) for i in range(GROUP)]
+            for h in range(4):
+                total = running[4 * GROUP * g + h]
+                for i in range(GROUP):
+                    s = g * GROUP + i
+                    here = tables[FAR_TARGET + e * CAP + s]
+                    same = (here == tables[FAR_TARGET + e * CAP + s - 1]).astype(jnp.int32)
+                    total = total * same.astype(F32) + terms[i][h * QUARTER : (h + 1) * QUARTER]
+                    running[4 * (s + 1) + h] = total
+
+        for d in ORDER:
+            for ax in range(2):
+
+                @pl.loop(0, 4)
+                def _(q):
+                    place = (q * 4 + lax.rem(self.x + d, 4)) if ax == 0 else (lax.rem(self.y + d, 4) * 4 + q)
+                    first = FAR_LAST + e * TARGETS + place * 2
+                    for ref, core in ((self.give, 1 - self.k), (self.own, self.k)):
+                        spot = 4 * tables[first + core] + 2 * ax
+                        for h in range(2):
+                            ref[ax, d, q, h * QUARTER : (h + 1) * QUARTER, :] = running[spot + h].astype(BF16)
+
+                self.pair_copy(ax, d).start()
 
     def arrived(self, ax, d):
-        if self.own is not None:
-            self.local_copy(ax, d).wait()
-        self.pair_copy(ax, d).wait()
+        self.pair_copy(ax, d).wait_recv()
+
+    def gave(self):
+        if not self.given:
+            for d in ORDER:
+                for ax in range(2):
+                    self.pair_copy(ax, d).wait_send()
+        self.given = True
+
+    def out(self, ax, d):
+        return self.sent.at[ax, d if self.own is not None else d - 1]
 
     def mine(self, ax, d, q):
         if self.own is not None:
@@ -311,7 +341,7 @@
         low = 2 * side if part == 0 else 2 * side if part == 2 else 2 - 2 * side
         rows = pl.ds(low, 2)
         return pltpu.make_async_remote_copy(
-            src_ref=self.across.at[ax, rows] if part == 0 else self.s1.at[ax, side, rows],
+            src_ref=self.out(ax, 2 if part == 0 else SIDES[side]).at[rows],
             dst_ref=self.passing.at[ax, side] if part == 0 else self.r1.at[ax, side, rows],
             send_sem=self.msem.at[ax, side, part, 0],
             recv_sem=self.msem.at[ax, side, part, 1],
@@ -336,7 +366,7 @@
 
                 @pl.loop(2 * side, 2 * side + 2)
                 def _(q):
-                    self.across[ax, q] = self.mine(ax, 2, q).astype(BF16)
+                    self.out(ax, 2)[q] = self.mine(ax, 2, q).astype(BF16)
 
                 self.ring_copy(ax, side, 0).start()
 
@@ -347,7 +377,7 @@
 
                 @pl.loop(2 - 2 * side, 4 - 2 * side)
                 def _(q):
-                    self.s1[ax, side, q] = self.mine(ax, SIDES[side], q).astype(BF16)
+                    self.out(ax, SIDES[side])[q] = self.mine(ax, SIDES[side], q).astype(BF16)
 
                 self.ring_copy(ax, side, 1).start()
 
@@ -360,7 +390,7 @@
                 def _(p):
                     q = 2 * side + p
                     total = self.mine(ax, SIDES[side], q) + self.passing[ax, side, p].astype(F32)
-                    self.s1[ax, side, q] = total.astype(BF16)
+                    self.out(ax, SIDES[side])[q] = total.astype(BF16)
 
                 self.ring_copy(ax, side, 2).start()
 
@@ -392,6 +422,7 @@
         return total
 
     def finish(self):
+        self.gave()
         for ax in range(2):
             for side in range(2):
                 for part in range(3):
@@ -411,10 +442,12 @@
     pl.semaphore_wait(barrier, len(partners))
 
 
-def exchange_kernel(slots, far, tables_in, loads_in, dense, received, results, sums0, sums1, *scratch):
+def exchange_kernel(slots, tables_in, loads, dense, received, results, sums0, sums1, *scratch):
     sums = (sums0, sums1)
-    planes = [PlaneSum((far.at[e], far.at[e]), scratch[12 * e : 12 * e + 12], True) for e in range(len(FAR))]
-    tables, loads, turned, blocks, running, zsem, lsem, dsem = scratch[36:]
+    gives = scratch[30:32]
+    planes = [PlaneSum(None, scratch[10 * e : 10 * e + 10], gives[e % 2]) for e in range(len(FAR))]
+    far_slots = scratch[32:35]
+    tables, turned, blocks, running, zsem, lsem, dsem = scratch[35:]
     b = lax.axis_index("blk")
     c = lax.axis_index("col")
 
@@ -423,12 +456,16 @@
 
     own_slots = pltpu.make_async_copy(slots.at[0], received.at[pl.ds(len(NEAR) * CAP, CAP)], lsem.at[0])
     table_copy = pltpu.make_async_copy(tables_in, tables, lsem.at[1])
-    load_copy = pltpu.make_async_copy(loads_in, loads, lsem.at[2])
+    far_copies = [
+        pltpu.make_async_copy(slots.at[d], far_slots[e], lsem.at[2 + e]) for e, d in enumerate(FAR)
+    ]
     part = DENSE // PIECES
     dense_copies = [
         pltpu.make_async_copy(dense.at[pl.ds(p * part, part)], blocks.at[pl.ds(p * part, part)], dsem.at[p])
         for p in range(PIECES)
     ]
+    for copy in [table_copy] + far_copies:
+        copy.start()
     greet(planes[0].partners() + [above(d) for d in NEAR])
     moves = [
         pltpu.make_async_remote_copy(
@@ -441,24 +478,21 @@
         )
         for i, d in enumerate(NEAR)
     ]
-    for plane in planes[:1]:
-        plane.begin()
     for move in moves:
         move.start()
-    for plane in planes[1:]:
-        plane.begin()
-    for copy in [table_copy, load_copy, own_slots] + dense_copies:
+    for copy in [own_slots] + dense_copies:
         copy.start()
     received[NULL] = jnp.zeros((2 * RANK, LEAF), BF16)
 
-    def dense_sums(half):
-        running[0] = jnp.zeros((HALF, LEAF), F32)
+    def dense_sums(part):
+        low = part * QUARTER
+        running[0] = jnp.zeros((QUARTER, LEAF), F32)
 
         @pl.loop(0, DENSE // GROUP)
         def _(g):
             terms = [
                 jnp.dot(
-                    turned[tables[SOURCED + g * GROUP + i], half * HALF : (half + 1) * HALF, :],
+                    turned[tables[SOURCED + g * GROUP + i], low : low + QUARTER, :],
                     blocks[tables[ORDERED + g * GROUP + i]],
                     preferred_element_type=F32,
                 )
@@ -466,32 +500,37 @@
             ]
             total = running[g * GROUP]
             for i in range(GROUP):
-                total = total * tables[SAME + g * GROUP + i].astype(F32) + terms[i]
+                here = tables[TARGETED + g * GROUP + i]
+                same = (here == tables[TARGETED + g * GROUP + i - 1]).astype(jnp.int32)
+                total = total * same.astype(F32) + terms[i]
                 running[g * GROUP + i + 1] = total
 
         @pl.loop(0, TARGETS)
         def _(t):
-            sums[half][t] = running[tables[LAST + t]] * tables[HAS + t].astype(F32)
-
-
-    planes[0].opposite()
-    planes[0].beside()
-    planes[1].opposite()
-    planes[1].beside()
-    planes[0].relay()
-    planes[2].opposite()
-    planes[2].beside()
-    load_copy.wait()
+            sums[low // HALF][t, low % HALF : low % HALF + QUARTER, :] = running[tables[LAST + t]] * tables[HAS + t].astype(F32)
+
+
     table_copy.wait()
+    for e, plane in enumerate(planes):
+        far_copies[e].wait()
+        if e == 2:
+            planes[0].gave()
+        plane.form(tables, e, far_slots[e], running)
+        plane.opposite()
+        plane.beside()
+        if e == 1:
+            planes[0].relay()
     for s in range(SOURCES):
         turned[s] = loads[s].T
     planes[1].relay()
     for copy in dense_copies:
         copy.wait()
     dense_sums(0)
+    dense_sums(1)
     planes[0].turn()
     planes[2].relay()
-    dense_sums(1)
+    dense_sums(2)
+    dense_sums(3)
     planes[1].turn()
     planes[2].turn()
     for e, plane in enumerate(planes):
@@ -504,7 +543,7 @@
         move.wait()
 
 
-def exchange(slots, far, tables, loads, dense):
+def exchange(slots, tables, loads, dense):
     scratch = []
     for _ in FAR:
         scratch += reduce_scratch(BF16, True)
@@ -516,24 +555,25 @@
             jax.ShapeDtypeStruct((TARGETS, HALF, LEAF), F32),
             jax.ShapeDtypeStruct((TARGETS, HALF, LEAF), F32),
         ),
-        in_specs=[spec(pl.ANY)] * 5,
+        in_specs=[spec(pl.ANY), spec(pl.ANY), spec(pltpu.VMEM), spec(pl.ANY)],
         out_specs=(spec(pltpu.VMEM),) * 4,
         scratch_shapes=scratch
+        + [pltpu.VMEM((2, 4, 4, HALF, LEAF), BF16)] * 2
+        + [pltpu.VMEM((CAP, 2 * RANK, LEAF), BF16)] * len(FAR)
         + [
             pltpu.SMEM((TABLE,), jnp.int32),
-            pltpu.VMEM((SOURCES, LEAF, CASES), BF16),
             pltpu.VMEM((SOURCES, CASES, LEAF), BF16),
             pltpu.VMEM((DENSE, LEAF, LEAF), BF16),
-            pltpu.VMEM((DENSE + 1, HALF, LEAF), F32),
+            pltpu.VMEM((4 * (CAP + 1), QUARTER, LEAF), F32),
             pltpu.SemaphoreType.DMA((len(NEAR), 2)),
             pltpu.SemaphoreType.DMA((5,)),
             pltpu.SemaphoreType.DMA((PIECES,)),
         ],
         compiler_params=pltpu.CompilerParams(
-            collective_id=1, has_side_effects=True, vmem_limit_bytes=42 * MIB
+            collective_id=1, has_side_effects=True, vmem_limit_bytes=40 * MIB
         ),
         name="exchange",
-    )(slots, far, tables, loads, dense)
+    )(slots, tables, loads, dense)
 
 
 def gather_kernel(tables, received, in0, in1, sums0, sums1):
@@ -559,8 +599,8 @@
 
 
 def final_kernel(source0, source1, results, out, *scratch):
-    own = PlaneSum((source0, source1), scratch[:11], False)
-    landed, zsem = scratch[11:]
+    own = PlaneSum((source0, source1), scratch[:10], None)
+    landed, zsem = scratch[10:]
     b = lax.axis_index("blk")
     c = lax.axis_index("col")
 
@@ -628,12 +668,10 @@
     target = block_target.reshape(PLANES, LOW)
     left = left_factors.reshape(LOW, RANK, LEAF)
     right = right_factors.reshape(LOW, RANK, LEAF)
-    slots, far, tables = pack(
+    slots, tables = pack(
         owner, source, target, dense_source.reshape(DENSE), dense_target.reshape(DENSE), loads, left, right
     )
-    received, results, *sums = exchange(
-        slots, far.reshape(len(FAR), 4, 4, 2, CASES, LEAF), tables, loads, dense_blocks.reshape(DENSE, LEAF, LEAF)
-    )
+    received, results, *sums = exchange(slots, tables, loads, dense_blocks.reshape(DENSE, LEAF, LEAF))
     sums = gather(tables, received, sums)
     return final(sums, results)
 

time: 92.7 us -> 90.9 us (0.981)
  Pallas kernels: 90 us -> 88.2 us
    pallas_call x1, Pallas kernels: 12.7 us -> 8.39 us  [pack(): pl.pallas_call(pack_kernel, out_shape=(jax.ShapeDtypeStruct((PLANES, CAP,...]
    pallas_call x1, Pallas kernels: 48.5 us -> 51 us  [exchange(): pl.pallas_call(exchange_kernel, out_shape=(jax.ShapeDtypeStruct((NULL + 1...]
    pallas_call x1, Pallas kernels: 5.63 us -> 3.29 us  [gather(): pl.pallas_call(gather_kernel, out_shape=(jax.ShapeDtypeStruct((TARGETS, H...]
    pallas_call x1, Pallas kernels: 23.2 us -> 25.4 us  [final(): pl.pallas_call(final_kernel, out_shape=jax.ShapeDtypeStruct((LEAF, CASES)...]
where the time goes in v3:
time: 90.9 us; the launch traced here: 90.8 us
  Pallas kernels  88.2 us (97%)
  local copies, waits for them, and re-layouts  2.56 us (3%)
    pallas_call x1, Pallas kernels, exchange(): pl.pallas_call(exchange_kernel, out_shape=(jax.ShapeDtypeStruct((NULL + 1...  51 us
    pallas_call x1, Pallas kernels, final(): pl.pallas_call(final_kernel, out_shape=jax.ShapeDtypeStruct((LEAF, CASES)...  25.4 us
    pallas_call x1, Pallas kernels, pack(): pl.pallas_call(pack_kernel, out_shape=(jax.ShapeDtypeStruct((PLANES, CAP,...  8.39 us
    pallas_call x1, Pallas kernels, gather(): pl.pallas_call(gather_kernel, out_shape=(jax.ShapeDtypeStruct((TARGETS, H...  3.29 us
    unnamed x5, local copies, waits for them, and re-layouts  2.56 us

profile of v3, /device:TPU:1, one launch (start us, length us, event | category | flops | bytes accessed | tf_op | source)
XLA Modules:
  0.0 90.8 jit_solution(11296538998622240200)
XLA Ops:
  0.0 8.4 %pack.1 = (bf16[8,16,64,256]{3,2,1,0:T(8,128)(2,1)}, s32[768]{0:T(1024)}) custom-call(s32[8,64]{1,0:T(8,128)} %bitcast.18, s32[8,64]{1,0:T(8,128)} %bitcast.19, s32[8,64]{1,0:T(8,128)} %bitcast.20, s32[60]{0:T(128)} %bitcast.21, s32[60]{0:T(128)} %bitcast.22, bf16[8,256,256]{2,1,0:T(8,128)(2,1)} %bitcast.13, bf16[64,32,256]{2,1,0:T(8,128)(2,1)} %bitcast.16, ...), custom_call_target="tpu_custom_call" | custom-call | tf_op jit(solution)/shard_map/pack/pallas_call | solution.py:198
  8.4 0.0 copy-start
  8.4 1.2 %copy-done = bf16[2048,256]{1,0:T(8,128)(2,1)S(1)} copy-done((bf16[2048,256]{1,0:T(8,128)(2,1)S(1)}, bf16[2048,256]{1,0:T(8,128)(2,1)}, u32[]{:S(2)}) %copy-start) | copy-done | bytes 1048600
  9.6 0.0 copy-start.1
  9.6 0.7 copy-done.1
  10.3 51.0 %exchange.1 = (bf16[81,64,256]{2,1,0:T(8,128)(2,1)S(1)}, bf16[3,256,256]{2,1,0:T(8,128)(2,1)S(1)}, f32[32,128,256]{2,1,0:T(8,128)S(1)}, f32[32,128,256]{2,1,0:T(8,128)S(1)}) custom-call(bf16[8,16,64,256]{3,2,1,0:T(8,128)(2,1)} %get-tuple-element.14.slots, s32[768]{0:T(1024)S(1)} %copy-done.1, bf16[8,256,256]{2,1,0:T(8,128)(2,1)S(1)} %bitcast.14, ...), custom_call_target="tpu_custom_call" | custom-call | tf_op jit(solution)/shard_map/exchange/pallas_call | solution.py:550
  61.4 3.3 %gather.1 = (f32[32,128,256]{2,1,0:T(8,128)S(1)}, f32[32,128,256]{2,1,0:T(8,128)S(1)}) custom-call(s32[768]{0:T(1024)S(1)} %copy-done.1, bf16[81,64,256]{2,1,0:T(8,128)(2,1)S(1)} %get-tuple-element.15.received, f32[32,128,256]{2,1,0:T(8,128)S(1)} %get-tuple-element.16.in0, ...), custom_call_target="tpu_custom_call", output_to_operand_aliasing={{0}: (2, {}), {1}: (3, {})} | custom-call | tf_op jit(solution)/shard_map/gather/pallas_call | solution.py:590
  64.7 25.4 %final.1 = bf16[256,256]{1,0:T(8,128)(2,1)S(1)} custom-call(f32[4,4,2,128,256]{4,3,2,1,0:T(8,128)S(1)} %bitcast.11, f32[4,4,2,128,256]{4,3,2,1,0:T(8,128)S(1)} %bitcast.12, bf16[3,256,256]{2,1,0:T(8,128)(2,1)S(1)} %get-tuple-element.20.results), custom_call_target="tpu_custom_call" | custom-call | tf_op jit(solution)/shard_map/final/pallas_call | solution.py:640
  90.1 0.7 copy.15
Async XLA Ops:
  8.4 1.2 %copy-start = (bf16[2048,256]{1,0:T(8,128)(2,1)S(1)}, bf16[2048,256]{1,0:T(8,128)(2,1)}, u32[]{:S(2)}) copy-start(bf16[2048,256]{1,0:T(8,128)(2,1)} %param.9) | copy-start | bytes 3145732
  9.6 0.7 copy-start.1

commit v4 on v3

--- a/solution.py
+++ b/solution.py
@@ -17,6 +17,7 @@
 CAP = 16
 PLANES = 8
 GROUP = 4
+NEAR_GROUP = 8
 PIECES = 4
 ORDERED = 0
 SOURCED = 64
@@ -123,25 +124,10 @@
     for t in range(TARGETS):
         tables[HAS + t] = jnp.minimum(tables[HAS + t], 1)
 
-    length = jnp.int32(0)
-    for i, d in enumerate(NEAR + (0,)):
-        sender = lax.rem(b - d + PLANES, PLANES)
-
-        def scan(n, carry, i=i, sender=sender):
-            length, rank = carry
-            tables[IDS + length] = target[sender, n]
-            tables[SPOTS + length] = i * CAP + rank
-            step = (owner[sender, n] == b).astype(jnp.int32)
-            return length + step, rank + step
-
-        length, _ = lax.fori_loop(0, LOW, scan, (length, jnp.int32(0)), unroll=8)
-    for j in range(GROUP):
-        tables[IDS + length + j] = 0
-        tables[SPOTS + length + j] = NULL
-    tables[LENGTH] = length
-
     for copy in large:
         copy.wait()
+
+    senders = [lax.rem(b - d + PLANES, PLANES) for d in NEAR + (0,)]
 
     def one(n, carry):
         d = lax.rem(owner[b, n] - b + PLANES, PLANES)
@@ -151,9 +137,20 @@
         coefficients = jnp.dot(left[n], loads[source[b, n]], preferred_element_type=F32)
         slots[d, r, :RANK, :] = right[n]
         slots[d, r, RANK:, :] = coefficients.astype(BF16)
-        return carry
-
-    lax.fori_loop(0, LOW, one, 0, unroll=8)
+        length, *ranks = carry
+        for i, sender in enumerate(senders):
+            tables[IDS + length] = target[sender, n]
+            tables[SPOTS + length] = i * CAP + ranks[i]
+            step = (owner[sender, n] == b).astype(jnp.int32)
+            length = length + step
+            ranks[i] = ranks[i] + step
+        return (length, *ranks)
+
+    length, *_ = lax.fori_loop(0, LOW, one, (jnp.int32(0),) * (2 + len(NEAR)), unroll=8)
+    for j in range(NEAR_GROUP):
+        tables[IDS + length + j] = 0
+        tables[SPOTS + length + j] = NULL
+    tables[LENGTH] = length
     whole = pltpu.make_async_copy(slots, slots_out, vsem.at[0])
     whole.start()
 
@@ -577,11 +574,11 @@
 
 
 def gather_kernel(tables, received, in0, in1, sums0, sums1):
-    @pl.loop(0, lax.div(tables[LENGTH] + GROUP - 1, GROUP))
+    @pl.loop(0, lax.div(tables[LENGTH] + NEAR_GROUP - 1, NEAR_GROUP))
     def _(g):
-        terms = [contribution(received[tables[SPOTS + g * GROUP + i]]) for i in range(GROUP)]
-        for i in range(GROUP):
-            t = tables[IDS + g * GROUP + i]
+        terms = [contribution(received[tables[SPOTS + g * NEAR_GROUP + i]]) for i in range(NEAR_GROUP)]
+        for i in range(NEAR_GROUP):
+            t = tables[IDS + g * NEAR_GROUP + i]
             sums0[t] += terms[i][:HALF]
             sums1[t] += terms[i][HALF:]
 

time: 90.9 us -> 87.4 us (0.961)
  Pallas kernels: 88.2 us -> 84.6 us
    pallas_call x1, Pallas kernels: 25.4 us -> 21 us  [final(): pl.pallas_call(final_kernel, out_shape=jax.ShapeDtypeStruct((LEAF, CASES)...]
    pallas_call x1, Pallas kernels: 3.29 us -> 5.47 us  [gather(): pl.pallas_call(gather_kernel, out_shape=(jax.ShapeDtypeStruct((TARGETS, H...]
    pallas_call x1, Pallas kernels: 8.39 us -> 7.07 us  [pack(): pl.pallas_call(pack_kernel, out_shape=(jax.ShapeDtypeStruct((PLANES, CAP,...]
where the time goes in v4:
time: 87.4 us; the launch traced here: 87.2 us
  Pallas kernels  84.6 us (97%)
  local copies, waits for them, and re-layouts  2.56 us (3%)
    pallas_call x1, Pallas kernels, exchange(): pl.pallas_call(exchange_kernel, out_shape=(jax.ShapeDtypeStruct((NULL + 1...  51.1 us
    pallas_call x1, Pallas kernels, final(): pl.pallas_call(final_kernel, out_shape=jax.ShapeDtypeStruct((LEAF, CASES)...  21 us
    pallas_call x1, Pallas kernels, pack(): pl.pallas_call(pack_kernel, out_shape=(jax.ShapeDtypeStruct((PLANES, CAP,...  7.07 us
    pallas_call x1, Pallas kernels, gather(): pl.pallas_call(gather_kernel, out_shape=(jax.ShapeDtypeStruct((TARGETS, H...  5.47 us
    unnamed x5, local copies, waits for them, and re-layouts  2.56 us

profile of v4, /device:TPU:1, one launch (start us, length us, event | category | flops | bytes accessed | tf_op | source)
XLA Modules:
  0.0 87.2 jit_solution(8191317524929621790)
XLA Ops:
  0.0 7.1 %pack.1 = (bf16[8,16,64,256]{3,2,1,0:T(8,128)(2,1)}, s32[768]{0:T(1024)}) custom-call(s32[8,64]{1,0:T(8,128)} %bitcast.18, s32[8,64]{1,0:T(8,128)} %bitcast.19, s32[8,64]{1,0:T(8,128)} %bitcast.20, s32[60]{0:T(128)} %bitcast.21, s32[60]{0:T(128)} %bitcast.22, bf16[8,256,256]{2,1,0:T(8,128)(2,1)} %bitcast.13, bf16[64,32,256]{2,1,0:T(8,128)(2,1)} %bitcast.16, ...), custom_call_target="tpu_custom_call" | custom-call | tf_op jit(solution)/shard_map/pack/pallas_call | solution.py:195
  7.1 0.0 copy-start
  7.1 1.2 %copy-done = bf16[2048,256]{1,0:T(8,128)(2,1)S(1)} copy-done((bf16[2048,256]{1,0:T(8,128)(2,1)S(1)}, bf16[2048,256]{1,0:T(8,128)(2,1)}, u32[]{:S(2)}) %copy-start) | copy-done | bytes 1048600
  8.3 0.0 copy-start.1
  8.3 0.7 copy-done.1
  9.0 51.1 %exchange.1 = (bf16[81,64,256]{2,1,0:T(8,128)(2,1)S(1)}, bf16[3,256,256]{2,1,0:T(8,128)(2,1)S(1)}, f32[32,128,256]{2,1,0:T(8,128)S(1)}, f32[32,128,256]{2,1,0:T(8,128)S(1)}) custom-call(bf16[8,16,64,256]{3,2,1,0:T(8,128)(2,1)} %get-tuple-element.14.slots, s32[768]{0:T(1024)S(1)} %copy-done.1, bf16[8,256,256]{2,1,0:T(8,128)(2,1)S(1)} %bitcast.14, ...), custom_call_target="tpu_custom_call" | custom-call | tf_op jit(solution)/shard_map/exchange/pallas_call | solution.py:547
  60.1 5.5 %gather.1 = (f32[32,128,256]{2,1,0:T(8,128)S(1)}, f32[32,128,256]{2,1,0:T(8,128)S(1)}) custom-call(s32[768]{0:T(1024)S(1)} %copy-done.1, bf16[81,64,256]{2,1,0:T(8,128)(2,1)S(1)} %get-tuple-element.15.received, f32[32,128,256]{2,1,0:T(8,128)S(1)} %get-tuple-element.16.in0, ...), custom_call_target="tpu_custom_call", output_to_operand_aliasing={{0}: (2, {}), {1}: (3, {})} | custom-call | tf_op jit(solution)/shard_map/gather/pallas_call | solution.py:587
  65.5 21.0 %final.1 = bf16[256,256]{1,0:T(8,128)(2,1)S(1)} custom-call(f32[4,4,2,128,256]{4,3,2,1,0:T(8,128)S(1)} %bitcast.11, f32[4,4,2,128,256]{4,3,2,1,0:T(8,128)S(1)} %bitcast.12, bf16[3,256,256]{2,1,0:T(8,128)(2,1)S(1)} %get-tuple-element.20.results), custom_call_target="tpu_custom_call" | custom-call | tf_op jit(solution)/shard_map/final/pallas_call | solution.py:637
  86.6 0.7 copy.15
Async XLA Ops:
  7.1 1.2 %copy-start = (bf16[2048,256]{1,0:T(8,128)(2,1)S(1)}, bf16[2048,256]{1,0:T(8,128)(2,1)}, u32[]{:S(2)}) copy-start(bf16[2048,256]{1,0:T(8,128)(2,1)} %param.9) | copy-start | bytes 3145732
  8.3 0.7 copy-start.1

commit v5 on v4

--- a/solution.py
+++ b/solution.py
@@ -286,13 +286,13 @@
         for h in range(4):
             running[h] = jnp.zeros((QUARTER, LEAF), F32)
 
-        @pl.loop(0, CAP // GROUP)
+        @pl.loop(0, CAP // NEAR_GROUP)
         def _(g):
-            terms = [contribution(slots[tables[FAR_ORDER + e * CAP + g * GROUP + i]]) for i in range(GROUP)]
+            terms = [contribution(slots[tables[FAR_ORDER + e * CAP + g * NEAR_GROUP + i]]) for i in range(NEAR_GROUP)]
             for h in range(4):
-                total = running[4 * GROUP * g + h]
-                for i in range(GROUP):
-                    s = g * GROUP + i
+                total = running[4 * NEAR_GROUP * g + h]
+                for i in range(NEAR_GROUP):
+                    s = g * NEAR_GROUP + i
                     here = tables[FAR_TARGET + e * CAP + s]
                     same = (here == tables[FAR_TARGET + e * CAP + s - 1]).astype(jnp.int32)
                     total = total * same.astype(F32) + terms[i][h * QUARTER : (h + 1) * QUARTER]
@@ -301,7 +301,7 @@
         for d in ORDER:
             for ax in range(2):
 
-                @pl.loop(0, 4)
+                @pl.loop(0, 4, unroll=4)
                 def _(q):
                     place = (q * 4 + lax.rem(self.x + d, 4)) if ax == 0 else (lax.rem(self.y + d, 4) * 4 + q)
                     first = FAR_LAST + e * TARGETS + place * 2

time: 87.4 us -> 87.3 us (level)
  no operation moved by 1% of the time
where the time goes in v5:
time: 87.3 us; the launch traced here: 86.8 us
  Pallas kernels  84.2 us (96%)
  local copies, waits for them, and re-layouts  2.56 us (3%)
    pallas_call x1, Pallas kernels, exchange(): pl.pallas_call(exchange_kernel, out_shape=(jax.ShapeDtypeStruct((NULL + 1...  50.7 us
    pallas_call x1, Pallas kernels, final(): pl.pallas_call(final_kernel, out_shape=jax.ShapeDtypeStruct((LEAF, CASES)...  21 us
    pallas_call x1, Pallas kernels, pack(): pl.pallas_call(pack_kernel, out_shape=(jax.ShapeDtypeStruct((PLANES, CAP,...  7.07 us
    pallas_call x1, Pallas kernels, gather(): pl.pallas_call(gather_kernel, out_shape=(jax.ShapeDtypeStruct((TARGETS, H...  5.47 us
    unnamed x5, local copies, waits for them, and re-layouts  2.56 us

profile of v5, /device:TPU:1, one launch (start us, length us, event | category | flops | bytes accessed | tf_op | source)
XLA Modules:
  0.0 86.8 jit_solution(1584873556190859703)
XLA Ops:
  0.0 7.1 %pack.1 = (bf16[8,16,64,256]{3,2,1,0:T(8,128)(2,1)}, s32[768]{0:T(1024)}) custom-call(s32[8,64]{1,0:T(8,128)} %bitcast.18, s32[8,64]{1,0:T(8,128)} %bitcast.19, s32[8,64]{1,0:T(8,128)} %bitcast.20, s32[60]{0:T(128)} %bitcast.21, s32[60]{0:T(128)} %bitcast.22, bf16[8,256,256]{2,1,0:T(8,128)(2,1)} %bitcast.13, bf16[64,32,256]{2,1,0:T(8,128)(2,1)} %bitcast.16, ...), custom_call_target="tpu_custom_call" | custom-call | tf_op jit(solution)/shard_map/pack/pallas_call | solution.py:195
  7.1 0.0 copy-start
  7.1 1.2 %copy-done = bf16[2048,256]{1,0:T(8,128)(2,1)S(1)} copy-done((bf16[2048,256]{1,0:T(8,128)(2,1)S(1)}, bf16[2048,256]{1,0:T(8,128)(2,1)}, u32[]{:S(2)}) %copy-start) | copy-done | bytes 1048600
  8.3 0.0 copy-start.1
  8.3 0.7 copy-done.1
  9.0 50.7 %exchange.1 = (bf16[81,64,256]{2,1,0:T(8,128)(2,1)S(1)}, bf16[3,256,256]{2,1,0:T(8,128)(2,1)S(1)}, f32[32,128,256]{2,1,0:T(8,128)S(1)}, f32[32,128,256]{2,1,0:T(8,128)S(1)}) custom-call(bf16[8,16,64,256]{3,2,1,0:T(8,128)(2,1)} %get-tuple-element.14.slots, s32[768]{0:T(1024)S(1)} %copy-done.1, bf16[8,256,256]{2,1,0:T(8,128)(2,1)S(1)} %bitcast.14, ...), custom_call_target="tpu_custom_call" | custom-call | tf_op jit(solution)/shard_map/exchange/pallas_call | solution.py:547
  59.7 5.5 %gather.1 = (f32[32,128,256]{2,1,0:T(8,128)S(1)}, f32[32,128,256]{2,1,0:T(8,128)S(1)}) custom-call(s32[768]{0:T(1024)S(1)} %copy-done.1, bf16[81,64,256]{2,1,0:T(8,128)(2,1)S(1)} %get-tuple-element.15.received, f32[32,128,256]{2,1,0:T(8,128)S(1)} %get-tuple-element.16.in0, ...), custom_call_target="tpu_custom_call", output_to_operand_aliasing={{0}: (2, {}), {1}: (3, {})} | custom-call | tf_op jit(solution)/shard_map/gather/pallas_call | solution.py:587
  65.2 21.0 %final.1 = bf16[256,256]{1,0:T(8,128)(2,1)S(1)} custom-call(f32[4,4,2,128,256]{4,3,2,1,0:T(8,128)S(1)} %bitcast.11, f32[4,4,2,128,256]{4,3,2,1,0:T(8,128)S(1)} %bitcast.12, bf16[3,256,256]{2,1,0:T(8,128)(2,1)S(1)} %get-tuple-element.20.results), custom_call_target="tpu_custom_call" | custom-call | tf_op jit(solution)/shard_map/final/pallas_call | solution.py:637
  86.2 0.7 copy.15
Async XLA Ops:
  7.1 1.2 %copy-start = (bf16[2048,256]{1,0:T(8,128)(2,1)S(1)}, bf16[2048,256]{1,0:T(8,128)(2,1)}, u32[]{:S(2)}) copy-start(bf16[2048,256]{1,0:T(8,128)(2,1)} %param.9) | copy-start | bytes 3145732
  8.3 0.7 copy-start.1
